TPU v7x, 256 devices: a whole 4x4x8 slice. The times are simulated.
256 devices in a mesh: dp: 16 (over x_lo, y, core), expert: 16 (over z, x_hi).
Axes of the slice: x: 4 (x_hi: 2, x_lo: 2; x = x_hi * 2 + x_lo), y: 4, z: 8, core: 2. Of those that a mesh axis runs over, the one named last changes fastest.
Arguments:
- tokens: bfloat16 [8192, 4096], P(('dp', 'expert')), may hold values from -6 to 6
- assign: int32 [256, 32], P(('dp', 'expert')), may hold values from 0 to 31, each once within a row
- w_in: bfloat16 [16, 4096, 4096], P('expert', None, 'dp'), may hold values from -0.09375 to 0.09375
- w_out: bfloat16 [16, 4096, 4096], P('expert', 'dp'), may hold values from -0.09375 to 0.09375
- cotangent: bfloat16 [8192, 4096], P(('dp', 'expert')), may hold values from -6 to 6
Outputs:
- output: bfloat16 [8192, 4096], P(('dp', 'expert'))
- grad_tokens: bfloat16 [8192, 4096], P(('dp', 'expert'))
- grad_in: bfloat16 [16, 4096, 4096], P('expert', None, 'dp')
- grad_out: bfloat16 [16, 4096, 4096], P('expert', 'dp')
Inputs may be any that keep to these rules, and one draw needn't show every extreme that they name: Each row of assign is a permutation of 0 .. 31.
All inputs are finite; a program needn't handle non-finite values.
Results may differ from a plain program's by a relative error of at most 0.0049.
Values may be sent and summed in bfloat16 or wider, within the bound.
A program may use at most 128 MiB of HBM per device.

v0:
```python
import jax
import jax.numpy as jnp
from jax import lax
from jax.sharding import PartitionSpec as P


def silu_slope(value):
    sig = jax.nn.sigmoid(value)
    return sig * (1.0 + value * (1.0 - sig))


def body(tokens, assign, w_in, w_out, cotangent):
    local_rows = tokens.shape[0]
    weight_in = w_in[0]
    weight_out = w_out[0]
    picker = (assign[0][:, None] == jnp.arange(local_rows, dtype=jnp.int32)[None, :]).astype(
        jnp.bfloat16
    )
    dealt_x = jnp.dot(picker, tokens, preferred_element_type=jnp.float32).astype(jnp.bfloat16)
    dealt_g = jnp.dot(picker, cotangent, preferred_element_type=jnp.float32).astype(jnp.bfloat16)
    sent_x, sent_g = (
        lax.all_to_all(dealt_x, "expert", split_axis=0, concat_axis=0, tiled=True),
        lax.all_to_all(dealt_g, "expert", split_axis=0, concat_axis=0, tiled=True),
    )
    width = tokens.shape[1]
    rows_x, rows_g = (
        lax.all_gather(sent_x, "dp", axis=0, tiled=True),
        lax.all_gather(sent_g, "dp", axis=0, tiled=True),
    )
    pre = jnp.dot(rows_x, weight_in, preferred_element_type=jnp.float32)
    act = jax.nn.silu(pre).astype(jnp.bfloat16)
    dact = lax.dot_general(
        rows_g, weight_out, (((1,), (1,)), ((), ())), preferred_element_type=jnp.float32
    )
    dpre = (dact * silu_slope(pre)).astype(jnp.bfloat16)
    out_term = jnp.dot(act, weight_out, preferred_element_type=jnp.float32)
    dx_term = lax.dot_general(
        dpre, weight_in, (((1,), (1,)), ((), ())), preferred_element_type=jnp.float32
    )
    summed = lax.psum_scatter(
        jnp.concatenate([out_term, dx_term], axis=1), "dp", scatter_dimension=0, tiled=True
    )
    out_rows = summed[:, :width].astype(jnp.bfloat16)
    dx_rows = summed[:, width:].astype(jnp.bfloat16)
    grad_w_in = lax.dot_general(
        rows_x, dpre, (((0,), (0,)), ((), ())), preferred_element_type=jnp.float32
    ).astype(jnp.bfloat16)
    grad_w_out = lax.dot_general(
        act, rows_g, (((0,), (0,)), ((), ())), preferred_element_type=jnp.float32
    ).astype(jnp.bfloat16)
    back_out, back_dx = (
        lax.all_to_all(out_rows, "expert", split_axis=0, concat_axis=0, tiled=True),
        lax.all_to_all(dx_rows, "expert", split_axis=0, concat_axis=0, tiled=True),
    )
    output = jnp.dot(picker.T, back_out, preferred_element_type=jnp.float32).astype(jnp.bfloat16)
    grad_tokens = jnp.dot(picker.T, back_dx, preferred_element_type=jnp.float32).astype(
        jnp.bfloat16
    )
    return (output, grad_tokens, grad_w_in[None], grad_w_out[None])


def solution(mesh):
    in_specs = (
        P(("dp", "expert"), None),
        P(("dp", "expert"), None),
        P("expert", None, "dp"),
        P("expert", "dp", None),
        P(("dp", "expert"), None),
    )
    out_specs = (
        P(("dp", "expert"), None),
        P(("dp", "expert"), None),
        P("expert", None, "dp"),
        P("expert", "dp", None),
    )
    return jax.shard_map(body, mesh=mesh, in_specs=in_specs, out_specs=out_specs, check_vma=False)
```

profile of v0, /device:TPU:1, one launch (start us, length us, event | category | flops | bytes accessed | tf_op | source)
XLA Modules:
  0.0 270.0 jit_solution(12103501682645420976)
XLA Ops:
  7.2 1.4 convolution_convert_fusion.5
  8.6 0.2 all_to_all.32
  8.8 23.4 %all_to_all.48 = bf16[16,2,4096]{2,1,0:T(2,128)(2,1)S(1)} all-to-all(bf16[16,2,4096]{2,1,0:T(2,128)(2,1)S(1)} %all_to_all.32), channel_id=1, replica_groups=mesh['dp'=16,'expert'=16] {'expert'}, dimensions={0} | all-to-all | bytes 524288 | tf_op jit(solution)/shard_map/all_to_all | solution.py:22
  32.2 0.8 all_to_all.34
  33.0 0.0 all-gather.5.cloned.1.call-start
  33.0 1.2 convolution_convert_fusion.4
  34.3 0.2 all_to_all.35
  34.5 14.4 %all_to_all.49 = bf16[16,2,4096]{2,1,0:T(2,128)(2,1)S(1)} all-to-all(bf16[16,2,4096]{2,1,0:T(2,128)(2,1)S(1)} %all_to_all.35), channel_id=1, replica_groups=mesh['dp'=16,'expert'=16] {'expert'}, dimensions={0} | all-to-all | bytes 524288 | tf_op jit(solution)/shard_map/all_to_all | solution.py:23
  48.9 0.8 all_to_all.37
  49.7 0.0 reduce-scatter.2.cloned.1.call-start
  49.8 21.7 %all-gather.3.cloned.1.call-done = bf16[512,4096]{1,0:T(8,128)(2,1)} async-done(((bf16[32,4096]{1,0:T(8,128)(2,1)}), bf16[512,4096]{1,0:T(8,128)(2,1)}) %all-gather.3.cloned.1.call-update) | async-done | bytes 4194320 | tf_op jit(solution)/shard_map/all_gather | solution.py:27
  71.5 4.1 %fusion.8 = f32[512,256]{1,0:T(8,128)S(1)} fusion(bf16[512,4096]{1,0:T(8,128)(2,1)} %all-gather.3.cloned.1.call-done, bf16[1,4096,256]{2,1,0:T(8,128)(2,1)} %param.7), kind=kOutput, calls=%fused_computation.15 | convolution fusion | flops 1073741824 | bytes 6815744 | tf_op jit(solution)/shard_map/dot_general | solution.py:30
  75.6 4.5 %fusion.4 = f32[512,4096]{1,0:T(8,128)} fusion(bf16[1,256,4096]{2,1,0:T(8,128)(2,1)S(1)} %copy-done, f32[512,256]{1,0:T(8,128)S(1)} %fusion.8), kind=kOutput, calls=%fused_computation.11 | convolution fusion | flops 1074397184 | bytes 11010048 | tf_op jit(solution)/shard_map/dot_general | solution.py:36
  80.1 33.4 %all-gather.5.cloned.1.call-done = bf16[512,4096]{1,0:T(8,128)(2,1)} async-done(((bf16[32,4096]{1,0:T(8,128)(2,1)}), bf16[512,4096]{1,0:T(8,128)(2,1)}) %all-gather.5.cloned.1.call-update) | async-done | bytes 4194320 | tf_op jit(solution)/shard_map/all_gather | solution.py:28
  113.5 3.6 %fusion.13 = bf16[512,256]{1,0:T(8,128)(2,1)S(1)} fusion(bf16[512,4096]{1,0:T(8,128)(2,1)} %all-gather.5.cloned.1.call-done, bf16[1,256,4096]{2,1,0:T(8,128)(2,1)S(1)} %copy-done, f32[512,256]{1,0:T(8,128)S(1)} %fusion.8), kind=kOutput, calls=%fused_computation.18 | convolution fusion | flops 1074921472 | bytes 7077888 | tf_op jit(solution)/shard_map/dot_general | solution.py:32
  117.2 1.3 fusion.6
  118.5 1.0 slice-done.1
  119.5 6.1 %pad_maximum_fusion = f32[512,8192]{1,0:T(8,128)} fusion(f32[512,4096]{1,0:T(8,128)S(1)} %fusion.6, f32[512,4096]{1,0:T(8,128)S(1)} %bitcast.30), kind=kLoop, calls=%fused_computation | loop fusion | flops 4194304 | bytes 33554432 | tf_op jit(solution)/shard_map/concatenate | solution.py:41
  125.6 99.2 %reduce-scatter.2.cloned.1.call-done = f32[32,8192]{1,0:T(8,128)} async-done(((f32[512,8192]{1,0:T(8,128)}), f32[32,8192]{1,0:T(8,128)}) %reduce-scatter.2.cloned.1.call-update) | async-done | bytes 1048592 | tf_op jit(solution)/shard_map/reduce_scatter | solution.py:40
  224.8 1.3 convert.4
  226.1 0.9 all_to_all.41
  227.0 9.2 %all-to-all-start.3 = ((bf16[16,2,4096]{2,1,0:T(2,128)(2,1)}), bf16[16,2,4096]{2,1,0:T(2,128)(2,1)S(1)}, u32[]{:S(2)}, u32[]{:S(2)}) async-start(bf16[16,2,4096]{2,1,0:T(2,128)(2,1)} %all_to_all.41), calls=%async_computation.4 | async-start | bytes 524288 | tf_op jit(solution)/shard_map/all_to_all | solution.py:53
  236.3 4.8 %fusion = bf16[1,4096,256]{2,1,0:T(8,128)(2,1)} fusion(bf16[512,4096]{1,0:T(8,128)(2,1)} %all-gather.3.cloned.1.call-done, bf16[512,256]{1,0:T(8,128)(2,1)S(1)} %fusion.13), kind=kOutput, calls=%fused_computation.3 | convolution fusion | flops 1074790400 | bytes 6553600 | tf_op jit(solution)/shard_map/dot_general | solution.py:45
  241.1 0.9 all_to_all.38
  242.0 5.4 %all-to-all-done.3 = bf16[16,2,4096]{2,1,0:T(2,128)(2,1)S(1)} async-done(((bf16[16,2,4096]{2,1,0:T(2,128)(2,1)}), bf16[16,2,4096]{2,1,0:T(2,128)(2,1)S(1)}, u32[]{:S(2)}, u32[]{:S(2)}) %all-to-all-start.3) | async-done | bytes 262176 | tf_op jit(solution)/shard_map/all_to_all | solution.py:53
  247.4 3.8 %all-to-all-start.2 = ((bf16[16,2,4096]{2,1,0:T(2,128)(2,1)}), bf16[16,2,4096]{2,1,0:T(2,128)(2,1)S(1)}, u32[]{:S(2)}, u32[]{:S(2)}) async-start(bf16[16,2,4096]{2,1,0:T(2,128)(2,1)} %all_to_all.38), calls=%async_computation.3 | async-start | bytes 524288 | tf_op jit(solution)/shard_map/all_to_all | solution.py:52
  251.2 4.8 %fusion.1 = bf16[1,256,4096]{2,1,0:T(8,128)(2,1)} fusion(bf16[512,4096]{1,0:T(8,128)(2,1)} %all-gather.5.cloned.1.call-done, f32[512,256]{1,0:T(8,128)S(1)} %fusion.8), kind=kOutput, calls=%fused_computation.4 | convolution fusion | flops 1075445760 | bytes 6815744 | tf_op jit(solution)/shard_map/dot_general | solution.py:48
  256.0 0.1 all_to_all.43
  256.1 1.0 convolution_convert_fusion.2
  257.2 5.2 %all-to-all-done.2 = bf16[16,2,4096]{2,1,0:T(2,128)(2,1)S(1)} async-done(((bf16[16,2,4096]{2,1,0:T(2,128)(2,1)}), bf16[16,2,4096]{2,1,0:T(2,128)(2,1)S(1)}, u32[]{:S(2)}, u32[]{:S(2)}) %all-to-all-start.2) | async-done | bytes 262176 | tf_op jit(solution)/shard_map/all_to_all | solution.py:52
  262.3 0.1 all_to_all.40
  262.4 1.0 convolution_convert_fusion.3
  (15 shorter events, 0.1 us)
Async XLA Ops:
  7.2 68.4 %copy-start = (bf16[1,256,4096]{2,1,0:T(8,128)(2,1)S(1)}, bf16[1,256,4096]{2,1,0:T(8,128)(2,1)}, u32[]{:S(2)}) copy-start(bf16[1,256,4096]{2,1,0:T(8,128)(2,1)} %param.8) | copy-start | bytes 6291460
  7.2 64.3 %all-gather.3.cloned.1.call-start = ((), (), s32[]{:S(2)}) async-start(), calls=%async_computation.5 | async-start | bytes 4456448 | tf_op jit(solution)/shard_map/all_gather | solution.py:27
  33.0 80.5 %all-gather.5.cloned.1.call-start = ((), (), s32[]{:S(2)}) async-start(), calls=%async_computation.6 | async-start | bytes 4456448 | tf_op jit(solution)/shard_map/all_gather | solution.py:28
  49.7 175.1 %reduce-scatter.2.cloned.1.call-start = ((), (), s32[]{:S(2)}) async-start(), calls=%async_computation.7 | async-start | bytes 17825792 | tf_op jit(solution)/shard_map/reduce_scatter | solution.py:40
  113.5 3.6 %copy-start.1 = (bf16[1,4096,256]{2,1,0:T(8,128)(2,1)S(1)}, bf16[1,4096,256]{2,1,0:T(8,128)(2,1)}, u32[]{:S(2)}) copy-start(bf16[1,4096,256]{2,1,0:T(8,128)(2,1)} %param.7) | copy-start | bytes 6291460
  113.5 5.0 %slice-start = ((s8[8388608]{0:T(1024)(128)(4,1)}), s8[4194304]{0:T(1024)(128)(4,1)S(1)}, s32[]{:S(2)}) async-start(s8[8388608]{0:T(1024)(128)(4,1)} %bitcast.29), calls=%async_computation.8 | async-start | bytes 8388608
  117.2 2.3 slice-start.1
  227.0 20.4 %all-to-all-start.3 = ((bf16[16,2,4096]{2,1,0:T(2,128)(2,1)}), bf16[16,2,4096]{2,1,0:T(2,128)(2,1)S(1)}, u32[]{:S(2)}, u32[]{:S(2)}) async-start(bf16[16,2,4096]{2,1,0:T(2,128)(2,1)} %all_to_all.41), calls=%async_computation.4 | async-start | bytes 524288 | tf_op jit(solution)/shard_map/all_to_all | solution.py:53
  242.0 14.1 %copy-start.2 = (s32[1,32]{1,0:T(1,128)S(1)}, s32[1,32]{1,0:T(1,128)}, u32[]{:S(2)}) copy-start(s32[1,32]{1,0:T(1,128)} %param.6) | copy-start | bytes 388
  247.4 14.9 %all-to-all-start.2 = ((bf16[16,2,4096]{2,1,0:T(2,128)(2,1)}), bf16[16,2,4096]{2,1,0:T(2,128)(2,1)S(1)}, u32[]{:S(2)}, u32[]{:S(2)}) async-start(bf16[16,2,4096]{2,1,0:T(2,128)(2,1)} %all_to_all.38), calls=%async_computation.3 | async-start | bytes 524288 | tf_op jit(solution)/shard_map/all_to_all | solution.py:52
Sparse Core Ops, SparseCore 0:
  33.1 38.3 all-gather.2
  73.9 39.5 all-gather.4
  125.7 99.0 reduce-scatter.1
where the time goes:
time: 274 us; the launch traced here: 270 us
  waiting for transfers between devices  165 us (60%)
  blocking collectives  37.8 us (14%)
  matrix products  27.9 us (10%)
  between operations  13.9 us (5%)
  starting transfers between devices  13.1 us (5%)
  other arithmetic  7.39 us (3%)
  local copies, waits for them, and re-layouts  4.98 us (2%)
    reduce_scatter x1, waiting for transfers between devices, body(): lax.psum_scatter(jnp.concatenate([out_term, dx_term], axis=1), 'dp', scat...  99.2 us
    all_gather x1, waiting for transfers between devices, body(): lax.all_gather(sent_g, 'dp', axis=0, tiled=True)  33.4 us
    all_to_all x1, blocking collectives, body(): lax.all_to_all(dealt_x, 'expert', split_axis=0, concat_axis=0, tiled=True)  23.4 us
    all_gather x1, waiting for transfers between devices, body(): lax.all_gather(sent_x, 'dp', axis=0, tiled=True)  21.7 us
    all_to_all x1, blocking collectives, body(): lax.all_to_all(dealt_g, 'expert', split_axis=0, concat_axis=0, tiled=True)  14.4 us
    all_to_all x1, starting transfers between devices, body(): lax.all_to_all(dx_rows, 'expert', split_axis=0, concat_axis=0, tiled=True)  9.25 us
    concatenate x1, other arithmetic, body(): jnp.concatenate([out_term, dx_term], axis=1)  6.12 us
  transfers between devices with their start and end apart: 5, of which 5 were waited for; matrix products, arithmetic and copies ran while one was open for 8% of the time, Pallas kernels for 0%

commit v1 on v0

v1 whole, which is shorter than its diff:
```python
import jax
import jax.numpy as jnp
from jax import lax
from jax.experimental import pallas as pl
from jax.experimental.pallas import tpu as pltpu
from jax.sharding import PartitionSpec as P

MESH = pl.DeviceIdType.MESH
D = 4096
HID = 256
TILE = 512
FOLD = 8
PART = 1024
EXPERTS = 16
SLOTS = [(dz, f) for dz in (0, 1, 7, 2, 6, 3, 5, 4) for f in (0, 1)]


def kernel(
    q_ref, tok_ref, cot_ref, win_hbm, wout_hbm,
    out_ref, dtok_ref, gin_hbm, gout_hbm,
    stack, a_send, a_recv, r_send, r_recv,
    xg, gg, win, wout, py, pd, sby, sbd,
    rhy, rfy, rxy, rhd, rfd, rxd,
    act, dpre, acc_a, acc_b, gin, gout,
    ssem, rsem, lsem,
):
    me = lax.axis_index("dp")
    ex = lax.axis_index("expert")
    xl, y, core = me // 8, (me // 2) % 4, me % 2
    z, xh = ex // 2, ex % 2

    def dev(xl, y, core):
        return xl * 8 + y * 2 + core

    y_up = (dev(xl, (y + 1) % 4, core), ex)
    y_dn = (dev(xl, (y + 3) % 4, core), ex)
    x_nb = (dev(1 - xl, y, core), ex)
    twin = (dev(xl, y, 1 - core), ex)

    def slot_peer(dz, f):
        xl2 = (1 - xl) if f else xl
        xh2 = (1 - xh) if f else xh
        return (dev(xl2, y, core), ((z + dz) % 8) * 2 + xh2)

    bar = pltpu.get_barrier_semaphore()
    everyone = [y_up, y_dn, x_nb, twin] + [slot_peer(*s) for s in SLOTS[1:]]
    for peer in everyone:
        pl.semaphore_signal(bar, inc=1, device_id=peer, device_id_type=MESH)

    w1 = pltpu.make_async_copy(win_hbm.at[0], win, lsem.at[0])
    w2 = pltpu.make_async_copy(wout_hbm.at[0], wout, lsem.at[1])
    w1.start()
    w2.start()

    count = [0]
    started = []

    def remote(src, dst, peer):
        i = count[0]
        count[0] += 1
        copy = pltpu.make_async_remote_copy(
            src_ref=src, dst_ref=dst, send_sem=ssem.at[i], recv_sem=rsem.at[i],
            device_id=peer, device_id_type=MESH,
        )
        copy.start()
        started.append(copy)
        return copy

    def dot(a, b):
        return jnp.dot(a, b, preferred_element_type=jnp.float32)

    def dot_t(a, b):
        return lax.dot_general(a, b, (((1,), (1,)), ((), ())), preferred_element_type=jnp.float32)

    def dot_l(a, b):
        return lax.dot_general(a, b, (((0,), (0,)), ((), ())), preferred_element_type=jnp.float32)

    for c in range(4):
        stack[pl.ds(c * 32, 32), :] = tok_ref[:, pl.ds(c * PART, PART)]
        stack[pl.ds(128 + c * 32, 32), :] = cot_ref[:, pl.ds(c * PART, PART)]
    a_send[...] = dot(q_ref[...], stack[...]).astype(jnp.bfloat16).reshape(EXPERTS, 16, PART)
    a_recv[0] = a_send[ex]

    pl.semaphore_wait(bar, len(everyone))

    deal = [None]
    for j, s in enumerate(SLOTS):
        if j:
            peer = slot_peer(*s)
            deal.append(remote(a_send.at[peer[1]], a_recv.at[j], peer))

    o = lax.broadcasted_iota(jnp.int32, (128, 128), 0)
    i = lax.broadcasted_iota(jnp.int32, (128, 128), 1)
    same = (o // 16 == i % 8) & ((o % 16) // 2 == i // 16) & (o % 2 == (i % 16) // 8)
    unfold = jnp.where(same, 1.0, 0.0).astype(jnp.bfloat16)

    def rows(k, s, dx, dy):
        return pl.ds(k * 256 + s * 128 + (dx * 4 + dy) * 16, 16)

    def arrive(k):
        for j in range(8 * k, 8 * k + 8):
            if j:
                deal[j].wait_recv()
        flat = a_recv[pl.ds(8 * k, 8)].reshape(128, PART)
        flat = dot(unfold, flat).astype(jnp.bfloat16)
        for c in range(4):
            xg[rows(k, 0, 0, 0), pl.ds(c * PART, PART)] = flat[c * 16:(c + 1) * 16]
            gg[rows(k, 0, 0, 0), pl.ds(c * PART, PART)] = flat[64 + c * 16:64 + (c + 1) * 16]

    HALF = (pl.ds(0, 2048), pl.ds(2048, 2048))

    class Gather:
        def __init__(self, k):
            self.k = k
            self.got = {}
            self.twins = []

        def send(self, ref, name, src, dst, peer, half=None):
            a, b = rows(self.k, 0, *src), rows(self.k, 0, *dst)
            if half is None:
                copy = remote(ref.at[a, :], ref.at[b, :], peer)
            else:
                copy = remote(ref.at[a, HALF[half]], ref.at[b, HALF[half]], peer)
            self.got[name, dst, half] = copy

        def wait(self, name, dst, half=None):
            self.got[name, dst, half].wait_recv()

        def share(self, ref, pos):
            a, b = rows(self.k, 0, *pos), rows(self.k, 1, *pos)
            self.twins.append(remote(ref.at[a, :], ref.at[b, :], twin))

        def spread(self, ref, name, dx):
            self.send(ref, name, (dx, 0), (dx, 3), y_up)
            self.send(ref, name, (dx, 0), (dx, 1), y_dn)

        def relay(self, ref, name, dx, dy):
            self.wait(name, (dx, dy))
            if dy == 3:
                self.send(ref, name, (dx, 3), (dx, 2), y_up, 0)
            else:
                self.send(ref, name, (dx, 1), (dx, 2), y_dn, 1)

        def cross(self, dy):
            self.send(gg, "g", (0, dy), (1, dy), x_nb)

        def e0(self):
            self.send(xg, "x", (0, 0), (1, 0), x_nb)
            self.spread(gg, "g", 0)
            self.cross(0)
            self.spread(xg, "x", 0)
            self.share(xg, (0, 0))
            self.share(gg, (0, 0))

        def e1(self):
            self.wait("x", (1, 0))
            self.spread(xg, "x", 1)
            self.share(xg, (1, 0))
            for dy in (3, 1):
                self.relay(gg, "g", 0, dy)
                self.cross(dy)
                self.share(gg, (0, dy))

        def e2(self):
            for dy in (3, 1):
                self.relay(xg, "x", 0, dy)
                self.share(xg, (0, dy))
            self.wait("g", (1, 0))
            self.share(gg, (1, 0))

        def e3(self):
            for dy in (3, 1):
                self.relay(xg, "x", 1, dy)
                self.share(xg, (1, dy))

        def e4(self):
            self.wait("g", (0, 2), 0)
            self.wait("g", (0, 2), 1)
            self.cross(2)
            self.share(gg, (0, 2))

        def e5(self):
            self.wait("g", (1, 3))
            self.share(gg, (1, 3))
            self.wait("x", (0, 2), 0)
            self.wait("x", (0, 2), 1)
            self.share(xg, (0, 2))
            self.wait("g", (1, 1))
            self.share(gg, (1, 1))
            self.wait("x", (1, 2), 0)
            self.wait("x", (1, 2), 1)
            self.share(xg, (1, 2))
            self.wait("g", (1, 2))
            self.share(gg, (1, 2))

        def e6(self):
            for copy in self.twins:
                copy.wait_recv()

    def chunk(k):
        return pl.ds(k * 256, 256)

    def hidden(k):
        acc_a[...] = jnp.zeros_like(acc_a)
        acc_b[...] = jnp.zeros_like(acc_b)

        @pl.loop(0, D // PART)
        def _(n):
            cols = pl.ds(pl.multiple_of(n * PART, PART), PART)
            acc_a[...] += dot(xg[chunk(k), cols], win[cols, :])
            acc_b[...] += dot_t(gg[chunk(k), cols], wout[:, cols])

        pre = acc_a[...]
        sig = jax.nn.sigmoid(pre)
        act[chunk(k), :] = (pre * sig).astype(jnp.bfloat16)
        dpre[chunk(k), :] = (acc_b[...] * (sig * (1.0 + pre * (1.0 - sig)))).astype(jnp.bfloat16)

    def add(ref, at, *others):
        total = ref[at].astype(jnp.float32)
        for other, where in others:
            total = total + other[where].astype(jnp.float32)
        ref[at] = total.astype(jnp.bfloat16)

    class Reduce:
        def __init__(self, k):
            self.k = k
            self.y2 = []
            self.d2 = []
            self.c = {}

        def pair(self, p, sb, h):
            far = pl.ds(self.k * 256 + 128, 128)
            return remote(p.at[far, HALF[h]], sb.at[pl.ds(self.k * 128, 128), HALF[h]], twin)

        def make_y(self):
            a = act[chunk(self.k), :]
            for h in range(2):

                @pl.loop(0, 4)
                def _(n):
                    cols = pl.ds(pl.multiple_of(h * 2048 + n * TILE, TILE), TILE)
                    py[chunk(self.k), cols] = dot(act[chunk(self.k), :], wout[:, cols]).astype(jnp.bfloat16)

                self.y2.append(self.pair(py, sby, h))

        def make_d(self):
            for h in range(2):

                @pl.loop(0, 4)
                def _(n):
                    cols = pl.ds(pl.multiple_of(h * 2048 + n * TILE, TILE), TILE)
                    pd[chunk(self.k), cols] = dot_t(dpre[chunk(self.k), :], win[cols, :]).astype(jnp.bfloat16)

                self.d2.append(self.pair(pd, sbd, h))

        def fold(self, p, sb, copies):
            for h in range(2):
                copies[h].wait_recv()

                @pl.loop(0, 4)
                def _(n):
                    cols = pl.ds(pl.multiple_of(h * 2048 + n * TILE, TILE), TILE)
                    add(p, (pl.ds(self.k * 256, 128), cols), (sb, (pl.ds(self.k * 128, 128), cols)))

        def at(self, dx, dy):
            return rows(self.k, 0, dx, dy)

        def far(self, p, rh, name, dx):
            src = self.at(dx, 2)
            for h, peer in ((0, y_up), (1, y_dn)):
                self.c[name, "h", dx, h] = remote(p.at[src, HALF[h]], rh.at[self.k, dx, :, HALF[h]], peer)

        def near(self, p, rh, rf, name, dx):
            for h, dy, peer in ((0, 1, y_up), (1, 3, y_dn)):
                self.c[name, "h", dx, h].wait_recv()
                at = self.at(dx, dy)
                add(p, (at, HALF[h]), (rh, (self.k, dx, slice(None), HALF[h])))
                self.c[name, "f", dx, h] = remote(p.at[at, :], rf.at[self.k, dx, h], peer)

        def own(self, p, rf, name, dx):
            for h in range(2):
                self.c[name, "f", dx, h].wait_recv()
            add(p, (self.at(dx, 0), slice(None)), (rf, (self.k, dx, 0)), (rf, (self.k, dx, 1)))

        def s3(self):
            self.fold(py, sby, self.y2)
            self.far(py, rhy, "y", 1)
            self.far(py, rhy, "y", 0)

        def s4(self):
            self.fold(pd, sbd, self.d2)
            for dy in (2, 1, 3, 0):
                self.c["d", "x", dy] = remote(pd.at[self.at(1, dy), :], rxd.at[self.k, dy], x_nb)

        def s5(self):
            self.near(py, rhy, rfy, "y", 1)
            self.near(py, rhy, rfy, "y", 0)

        def s6(self):
            for dy in (2, 1, 3, 0):
                self.c["d", "x", dy].wait_recv()
                add(pd, (self.at(0, dy), slice(None)), (rxd, (self.k, dy)))
                if dy == 2:
                    self.far(pd, rhd, "d", 0)

        def s7(self):
            self.own(py, rfy, "y", 1)
            self.c["y", "x"] = remote(py.at[self.at(1, 0), :], rxy.at[self.k], x_nb)
            self.own(py, rfy, "y", 0)

        def s8(self):
            self.near(pd, rhd, rfd, "d", 0)

        def s9(self):
            self.c["y", "x"].wait_recv()
            add(py, (self.at(0, 0), slice(None)), (rxy, (self.k,)))

        def s10(self):
            self.own(pd, rfd, "d", 0)

        def s11(self):
            at = self.at(0, 0)
            parts = [py[at, pl.ds(c * PART, PART)] for c in range(4)]
            parts += [pd[at, pl.ds(c * PART, PART)] for c in range(4)]
            flat = dot_l(unfold, jnp.concatenate(parts, axis=0)).astype(jnp.bfloat16)
            r_send[pl.ds(8 * self.k, 8)] = flat.reshape(8, 16, PART)
            if self.k == 0:
                r_recv[ex] = r_send[0]
            self.back = []
            for j in range(8 * self.k, 8 * self.k + 8):
                if j:
                    dz, f = SLOTS[j]
                    peer = slot_peer(8 - dz, f)
                    self.back.append(remote(r_send.at[j], r_recv.at[ex], peer))

    def grad_out(part):
        @pl.loop(0, 2)
        def _(n):
            cols = pl.ds(pl.multiple_of(part * 1024 + n * TILE, TILE), TILE)
            gout[:, cols] = dot_l(act[...], gg[:, cols]).astype(jnp.bfloat16)

    def grad_in(part):
        @pl.loop(0, 2)
        def _(n):
            cols = pl.ds(pl.multiple_of(part * 1024 + n * TILE, TILE), TILE)
            gin[cols, :] = dot_l(xg[:, cols], dpre[...]).astype(jnp.bfloat16)

    g0, g1 = Gather(0), Gather(1)
    r0, r1 = Reduce(0), Reduce(1)
    arrive(0)
    g0.e0()
    g0.e1()
    g0.e2()
    arrive(1)
    g0.e3()
    g1.e0()
    g0.e4()
    g0.e5()
    g1.e1()
    w1.wait()
    w2.wait()
    g0.e6()
    hidden(0)
    g1.e2()
    r0.make_y()
    g1.e3()
    r0.make_d()
    r0.s3()
    g1.e4()
    r0.s4()
    r0.s5()
    g1.e5()
    r0.s6()
    g1.e6()
    hidden(1)
    r0.s7()
    r0.s8()
    r1.make_y()
    r0.s9()
    r0.s10()
    r1.make_d()
    r1.s3()
    r0.s11()
    r1.s4()
    grad_out(0)
    grad_out(1)
    r1.s5()
    grad_out(2)
    r1.s6()
    grad_out(3)
    wo = pltpu.make_async_copy(gout, gout_hbm.at[0], lsem.at[2])
    wo.start()
    r1.s7()
    grad_in(0)
    r1.s8()
    grad_in(1)
    r1.s9()
    grad_in(2)
    r1.s10()
    r1.s11()
    grad_in(3)
    wi = pltpu.make_async_copy(gin, gin_hbm.at[0], lsem.at[3])
    wi.start()
    for copy in r0.back + r1.back:
        copy.wait_recv()
    back = dot_l(q_ref[...], r_recv[...].reshape(256, PART)).astype(jnp.bfloat16)
    for c in range(4):
        out_ref[:, pl.ds(c * PART, PART)] = back[c * 32:(c + 1) * 32]
        dtok_ref[:, pl.ds(c * PART, PART)] = back[128 + c * 32:128 + (c + 1) * 32]
    for copy in started:
        copy.wait_send()
    wo.wait()
    wi.wait()


COPIES = 2 * 15 + 2 * (17 + 16) + 2 * (4 + 8 + 9)


def body(tokens, assign, w_in, w_out, cotangent):
    bf = jnp.bfloat16
    folded = jnp.repeat(assign[0].reshape(EXPERTS, 2), FOLD, axis=1).reshape(256)
    where = jnp.tile(jnp.arange(FOLD, dtype=jnp.int32), 32) * 32 + folded
    q = (where[:, None] == jnp.arange(256, dtype=jnp.int32)[None, :]).astype(bf)

    vmem = pl.BlockSpec(memory_space=pltpu.VMEM)
    hbm = pl.BlockSpec(memory_space=pl.ANY)
    v = pltpu.VMEM
    return pl.pallas_call(
        kernel,
        out_shape=(
            jax.ShapeDtypeStruct(tokens.shape, bf),
            jax.ShapeDtypeStruct(tokens.shape, bf),
            jax.ShapeDtypeStruct(w_in.shape, bf),
            jax.ShapeDtypeStruct(w_out.shape, bf),
        ),
        in_specs=[vmem, vmem, vmem, hbm, hbm],
        out_specs=(vmem, vmem, hbm, hbm),
        scratch_shapes=[
            v((256, PART), bf),
            v((EXPERTS, 16, PART), bf), v((EXPERTS, 16, PART), bf),
            v((EXPERTS, 16, PART), bf), v((EXPERTS, 16, PART), bf),
            v((512, D), bf), v((512, D), bf),
            v((D, HID), bf), v((HID, D), bf),
            v((512, D), bf), v((512, D), bf),
            v((256, D), bf), v((256, D), bf),
            v((2, 2, 16, D), bf), v((2, 2, 2, 16, D), bf), v((2, 16, D), bf),
            v((2, 1, 16, D), bf), v((2, 1, 2, 16, D), bf), v((2, 4, 16, D), bf),
            v((512, HID), bf), v((512, HID), bf),
            v((256, HID), jnp.float32), v((256, HID), jnp.float32),
            v((D, HID), bf), v((HID, D), bf),
            pltpu.SemaphoreType.DMA((COPIES,)),
            pltpu.SemaphoreType.DMA((COPIES,)),
            pltpu.SemaphoreType.DMA((4,)),
        ],
        compiler_params=pltpu.CompilerParams(
            collective_id=0, has_side_effects=True, vmem_limit_bytes=56 * 2**20
        ),
        cost_estimate=pl.CostEstimate(
            flops=12 * 512 * D * HID, bytes_accessed=10 * 2**20, transcendentals=512 * HID
        ),
    )(q, tokens, cotangent, w_in, w_out)


def solution(mesh):
    in_specs = (
        P(("dp", "expert"), None),
        P(("dp", "expert"), None),
        P("expert", None, "dp"),
        P("expert", "dp", None),
        P(("dp", "expert"), None),
    )
    out_specs = (
        P(("dp", "expert"), None),
        P(("dp", "expert"), None),
        P("expert", None, "dp"),
        P("expert", "dp", None),
    )
    return jax.shard_map(body, mesh=mesh, in_specs=in_specs, out_specs=out_specs, check_vma=False)
```

time: 274 us -> 127 us (0.46)
  waiting for transfers between devices: 165 us -> 0 us
  Pallas kernels: 0 us -> 113 us
  blocking collectives: 37.8 us -> 0 us
  matrix products: 27.9 us -> 0 us
  between operations: 13.9 us -> 0.66 us
  starting transfers between devices: 13.1 us -> 0 us
  other arithmetic: 7.39 us -> 2.09 us
  local copies, waits for them, and re-layouts: 4.98 us -> 8.73 us
    pallas_call x0 -> x1, Pallas kernels: none -> 113 us  [body(): pl.pallas_call(kernel, out_shape=(jax.ShapeDtypeStruct(tokens.shape, bf),...]
    reduce_scatter x1 -> x0, waiting for transfers between devices: 99.2 us -> none  [body(): lax.psum_scatter(jnp.concatenate([out_term, dx_term], axis=1), 'dp', scat...]
    all_gather x2 -> x0, waiting for transfers between devices: 55.1 us -> none  [the longest x1 33.4 us: body(): lax.all_gather(sent_g, 'dp', axis=0, tiled=True)]
    all_to_all x2 -> x0, blocking collectives: 37.8 us -> none  [the longest x1 23.4 us: body(): lax.all_to_all(dealt_x, 'expert', split_axis=0, concat_axis=0, tiled=True)]
    dot_general x10 -> x0, matrix products: 27.9 us -> none  [the longest x1 4.82 us: body(): lax.dot_general(act, rows_g, (((0,), (0,)), ((), ())), preferred_element_...]
    all_to_all x2 -> x0, starting transfers between devices: 13 us -> none  [the longest x1 9.25 us: body(): lax.all_to_all(dx_rows, 'expert', split_axis=0, concat_axis=0, tiled=True)]
    all_to_all x2 -> x0, waiting for transfers between devices: 10.6 us -> none  [the longest x1 5.41 us: body(): lax.all_to_all(dx_rows, 'expert', split_axis=0, concat_axis=0, tiled=True)]
    unnamed x10 -> x7, local copies, waits for them, and re-layouts: 1.01 us -> 8.37 us
  transfers between devices with their start and end apart: 5 -> 0, of which waited for: 5 -> 0; matrix products, arithmetic and copies ran while one was open for 8% -> 0% of each run, Pallas kernels for 0% -> 0%
where the time goes in v1:
time: 127 us; the launch traced here: 125 us
  Pallas kernels  113 us (89%)
  local copies, waits for them, and re-layouts  8.73 us (7%)
  other arithmetic  2.09 us (2%)
    pallas_call x1, Pallas kernels, body(): pl.pallas_call(kernel, out_shape=(jax.ShapeDtypeStruct(tokens.shape, bf),...  113 us
    unnamed x7, local copies, waits for them, and re-layouts  8.37 us

profile of v1, /device:TPU:1, one launch (start us, length us, event | category | flops | bytes accessed | tf_op | source)
XLA Modules:
  0.0 124.7 jit_solution(5664794673727132429)
XLA Ops:
  0.6 0.5 broadcast.9
  1.1 1.3 %reduce.3 = s32[32]{0:T(128)S(1)} reduce(s32[1,32]{1,0:T(1,128)} %param.6, s32[]{:T(128)} %broadcast.9), dimensions={0}, to_apply=%param.6.reduce_sub_computation.3 | reduce | bytes 260 | tf_op args[1]
  2.5 0.1 reshape_squeeze.3
  2.5 0.1 broadcast_in_dim.2
  2.6 0.1 reshape_reshape.3
  2.7 0.1 mul.15
  2.8 0.8 fusion.q_ref
  3.6 113.2 %shard_map.84 = (bf16[32,4096]{1,0:T(8,128)(2,1)}, bf16[32,4096]{1,0:T(8,128)(2,1)}, bf16[1,4096,256]{2,1,0:T(8,128)(2,1)}, bf16[1,256,4096]{2,1,0:T(8,128)(2,1)}) custom-call(bf16[256,256]{1,0:T(8,128)(2,1)} %fusion.q_ref, bf16[32,4096]{1,0:T(8,128)(2,1)} %tok_ref.1, bf16[32,4096]{1,0:T(8,128)(2,1)} %cot_ref.1, bf16[1,4096,256]{2,1,0:T(8,128)(2,1)} %win_hbm.1, ...), custom_call_target="tpu_custom_call" | custom-call | flops 6442450944 | bytes 10485760 | tf_op jit(solution)/shard_map/pallas_call | solution.py:428
  116.9 1.7 %copy.13 = bf16[32,4096]{1,0:T(8,128)(2,1)} copy(bf16[32,4096]{1,0:T(8,128)(2,1)} %get-tuple-element.8) | data formatting | bytes 524288
  118.5 1.7 %copy.14 = bf16[32,4096]{1,0:T(8,128)(2,1)} copy(bf16[32,4096]{1,0:T(8,128)(2,1)} %get-tuple-element.9) | data formatting | bytes 524288
  120.2 0.0 copy-start
  120.2 3.2 %copy.15 = bf16[1,4096,256]{2,1,0:T(8,128)(2,1)} copy(bf16[1,4096,256]{2,1,0:T(8,128)(2,1)} %get-tuple-element.10) | data formatting | bytes 4194304
  123.4 0.0 copy-done
  123.4 1.3 %copy.16 = bf16[1,256,4096]{2,1,0:T(8,128)(2,1)} copy(bf16[1,256,4096]{2,1,0:T(8,128)(2,1)S(1)} %copy-done) | data formatting | bytes 4194304
  (2 shorter events, 0.0 us)
Async XLA Ops:
  120.2 3.2 %copy-start = (bf16[1,256,4096]{2,1,0:T(8,128)(2,1)S(1)}, bf16[1,256,4096]{2,1,0:T(8,128)(2,1)}, u32[]{:S(2)}) copy-start(bf16[1,256,4096]{2,1,0:T(8,128)(2,1)} %get-tuple-element.11) | copy-start | bytes 6291460

commit v2 on v0

v2 whole, which is shorter than its diff:
```python
import jax
import jax.numpy as jnp
from jax import lax
from jax.experimental import pallas as pl
from jax.experimental.pallas import tpu as pltpu
from jax.sharding import PartitionSpec as P

MESH = pl.DeviceIdType.MESH
D = 4096
HID = 256
TILE = 512
PART = 1024
EXPERTS = 16
SLOTS = [(0, 0), (0, 1), (1, 0), (1, 1), (7, 0), (7, 1), (2, 0), (6, 1)]
SLOTS += [(3, 0), (3, 1), (5, 0), (5, 1), (4, 0), (4, 1), (2, 1), (6, 0)]
LOW, HIGH = (0, 2048), (2048, 2048)
FIRST, MIDDLE, LAST = (0, 1024), (1024, 2048), (3072, 1024)


class Sent:
    def __init__(self, copy):
        self.copy = copy
        self.due = True

    def wait_recv(self):
        if self.due:
            self.copy.wait_recv()
        self.due = False


def kernel(
    assign_hbm, tok_hbm, cot_hbm, win_hbm, wout_hbm,
    out_ref, dtok_ref, gin, gout,
    assign_ref, stack, a_send, a_recv, r_send, r_recv,
    xg, gg, win, wout,
    own_y, own_d, far_y, far_d, sb_y, sb_d, st_y, st_d,
    rh_y, rf_y, rx_y, rh_d, rf_d, rx_d, rq_d,
    act, dpre, acc_a, acc_b,
    ssem, rsem, lsem,
):
    bf, f32 = jnp.bfloat16, jnp.float32
    me = lax.axis_index("dp")
    ex = lax.axis_index("expert")
    xl, y, core = me // 8, (me // 2) % 4, me % 2
    z, xh = ex // 2, ex % 2

    def dev(xl, y, core):
        return xl * 8 + y * 2 + core

    y_up = (dev(xl, (y + 1) % 4, core), ex)
    y_dn = (dev(xl, (y + 3) % 4, core), ex)
    x_nb = (dev(1 - xl, y, core), ex)
    twin = (dev(xl, y, 1 - core), ex)

    def slot_peer(dz, f):
        xl2 = (1 - xl) if f else xl
        xh2 = (1 - xh) if f else xh
        return (dev(xl2, y, core), ((z + dz) % 8) * 2 + xh2)

    bar = pltpu.get_barrier_semaphore()
    everyone = [slot_peer(*s) for s in SLOTS[:0:-1]] + [y_up, y_dn, x_nb, twin]
    for peer in everyone:
        pl.semaphore_signal(bar, inc=1, device_id=peer, device_id_type=MESH)

    load = [pltpu.make_async_copy(assign_hbm, assign_ref, lsem.at[0])]
    for n in range(8):
        src = (tok_hbm, cot_hbm)[n // 4].at[:, pl.ds(n % 4 * PART, PART)]
        load.append(pltpu.make_async_copy(src, stack.at[pl.ds(n * 32, 32), :], lsem.at[1 + n]))
    w1 = pltpu.make_async_copy(win_hbm.at[0], win, lsem.at[9])
    w2 = pltpu.make_async_copy(wout_hbm.at[0], wout, lsem.at[10])
    for copy in load + [w1, w2]:
        copy.start()

    count = [0]
    started = []

    def remote(src, dst, peer):
        i = count[0]
        count[0] += 1
        copy = pltpu.make_async_remote_copy(
            src_ref=src, dst_ref=dst, send_sem=ssem.at[i], recv_sem=rsem.at[i],
            device_id=peer, device_id_type=MESH,
        )
        copy.start()
        started.append(Sent(copy))
        return started[-1]

    def dot(a, b):
        return jnp.dot(a, b, preferred_element_type=f32)

    def dot_t(a, b):
        return lax.dot_general(a, b, (((1,), (1,)), ((), ())), preferred_element_type=f32)

    def dot_l(a, b):
        return lax.dot_general(a, b, (((0,), (0,)), ((), ())), preferred_element_type=f32)

    def iota(shape, dim):
        return lax.broadcasted_iota(jnp.int32, shape, dim)

    for copy in load:
        copy.wait()
    spread = jnp.where(iota((32, 256), 0) == iota((32, 256), 1) // 8, 1.0, 0.0).astype(bf)
    order = jnp.broadcast_to(assign_ref[...].astype(f32), (16, 32)).astype(bf)
    order = dot(order, spread)[0:1, :]
    row, col = iota((256, 256), 0), iota((256, 256), 1)
    hit = ((row // 32) == (col % 8)) & ((row % 32).astype(f32) == order)
    taken = jnp.where(hit, 1.0, 0.0).astype(bf)

    a_send[...] = dot_l(taken, stack[...]).astype(bf).reshape(EXPERTS, 16, PART)
    a_recv[0] = a_send[ex]

    o, i = iota((128, 128), 0), iota((128, 128), 1)
    same = (o // 16 == i % 8) & ((o % 16) // 2 == i // 16) & (o % 2 == (i % 16) // 8)
    unfold = jnp.where(same, 1.0, 0.0).astype(bf)

    pl.semaphore_wait(bar, len(everyone))

    deal = {}

    def deal_out(k):
        for j in range(8 * k, 8 * k + 8):
            if j:
                peer = slot_peer(*SLOTS[j])
                deal[j] = remote(a_send.at[peer[1]], a_recv.at[j], peer)

    def rows(k, s, dx, dy):
        return pl.ds(k * 256 + s * 128 + (dx * 4 + dy) * 16, 16)

    def block(dx, dy):
        return pl.ds((dx * 4 + dy) * 16, 16)

    def span(cols):
        return pl.ds(*cols)

    class Gather:
        def __init__(self, k):
            self.k = k
            self.got = {}
            self.twins = {True: [], False: []}

        def send(self, ref, src, dst, peer, cols=(0, D)):
            a, b = rows(self.k, 0, *src), rows(self.k, 0, *dst)
            copy = remote(ref.at[a, span(cols)], ref.at[b, span(cols)], peer)
            self.got.setdefault((ref is xg, dst), []).append(copy)

        def wait(self, ref, dst):
            for copy in self.got[ref is xg, dst]:
                copy.wait_recv()

        def share(self, ref, pos):
            a, b = rows(self.k, 0, *pos), rows(self.k, 1, *pos)
            self.twins[ref is xg].append(remote(ref.at[a, :], ref.at[b, :], twin))

        def round_y(self, ref, dx):
            self.send(ref, (dx, 0), (dx, 3), y_up)
            self.send(ref, (dx, 0), (dx, 1), y_dn)

        def arrive(self):
            k = self.k
            for j in range(8 * k, 8 * k + 8):
                if j:
                    deal[j].wait_recv()
            flat = a_recv[pl.ds(8 * k, 8)].reshape(128, PART)
            flat = dot(unfold, flat).astype(bf)
            for c in range(4):
                xg[rows(k, 0, 0, 0), pl.ds(c * PART, PART)] = flat[c * 16:(c + 1) * 16]
                gg[rows(k, 0, 0, 0), pl.ds(c * PART, PART)] = flat[64 + c * 16:64 + (c + 1) * 16]
            self.send(xg, (0, 0), (1, 0), x_nb)
            self.round_y(gg, 0)
            self.send(gg, (0, 0), (1, 0), x_nb)
            self.round_y(xg, 0)
            self.share(xg, (0, 0))
            self.share(gg, (0, 0))

        def take(self, ref, dx, dy):
            self.wait(ref, (dx, dy))
            side = ref is gg and dx == 1
            if dy == 3:
                self.send(ref, (dx, 3), (dx, 2), y_up, FIRST if side else LOW)
            elif dy == 1:
                self.send(ref, (dx, 1), (dx, 2), y_dn, LAST if side else HIGH)
            if ref is gg and dx == 0 and dy:
                self.send(gg, (0, dy), (1, dy), x_nb, MIDDLE if dy == 2 else (0, D))
            if ref is xg and dx == 1 and dy == 0:
                self.round_y(xg, 1)
            self.share(ref, (dx, dy))

        def whole(self, ref):
            for copy in self.twins[ref is xg]:
                copy.wait_recv()

    def chunk(k):
        return pl.ds(k * 256, 256)

    def hidden_x(k):
        acc_a[...] = jnp.zeros_like(acc_a)

        @pl.loop(0, D // PART)
        def _(n):
            cols = pl.ds(pl.multiple_of(n * PART, PART), PART)
            acc_a[...] += dot(xg[chunk(k), cols], win[cols, :])

    def hidden_g(k):
        acc_b[...] = jnp.zeros_like(acc_b)

        @pl.loop(0, D // PART)
        def _(n):
            cols = pl.ds(pl.multiple_of(n * PART, PART), PART)
            acc_b[...] += dot_t(gg[chunk(k), cols], wout[:, cols])

        pre = acc_a[...]
        sig = jax.nn.sigmoid(pre)
        act[chunk(k), :] = (pre * sig).astype(bf)
        dpre[chunk(k), :] = (acc_b[...] * (sig * (1.0 + pre * (1.0 - sig)))).astype(bf)

    class Reduce:
        def __init__(self, k, own, far, sb, st, rh, rf):
            self.k, self.own, self.far, self.sb, self.st = k, own, far, sb, st
            self.rh, self.rf = rh, rf
            self.pair = []
            self.half = {}
            self.full = {}

        def make(self, h, product):
            k = self.k

            @pl.loop(0, 4)
            def _(n):
                cols = pl.ds(pl.multiple_of(h * 2048 + n * TILE, TILE), TILE)
                t = product(k, cols)
                self.own[k, :, cols] = t[:128]
                self.far[k, :, cols] = t[128:].astype(bf)

            cols = span((LOW, HIGH)[h])
            self.pair.append(remote(self.far.at[k, :, cols], self.sb.at[k, :, cols], twin))

        def total(self, dst, dx, dy, cols, *others):
            @pl.loop(0, cols[1] // PART)
            def _(n):
                at = pl.ds(pl.multiple_of(cols[0] + n * PART, PART), PART)
                t = self.own[self.k, block(dx, dy), at] + self.sb[self.k, block(dx, dy), at].astype(f32)
                for other in others:
                    t = t + other[:, at].astype(f32)
                dst[:, at] = t.astype(bf)

        def stage(self, dx, dy):
            return self.st.at[self.k, dx * 4 + dy]

        def twins(self):
            for copy in self.pair:
                copy.wait_recv()

        def send_far(self, dx):
            self.twins()
            extra = (rx_d.at[self.k, 2],) if self is d[self.k] else ()
            if extra:
                cross[self.k, 2].wait_recv()
            st = self.stage(dx, 2)
            if extra:
                self.total(st, dx, 2, FIRST)
                self.total(st, dx, 2, MIDDLE, *extra)
                self.total(st, dx, 2, LAST)
            else:
                self.total(st, dx, 2, (0, D))
            for h, cols, peer in ((0, LOW, y_up), (1, HIGH, y_dn)):
                self.half[dx, h] = remote(st.at[:, span(cols)], self.rh.at[self.k, dx, :, span(cols)], peer)

        def send_near(self, dx, h):
            dy = (1, 3)[h]
            extra = ()
            if self is d[self.k]:
                cross[self.k, dy].wait_recv()
                extra = (rx_d.at[self.k, dy],)
            self.half[dx, h].wait_recv()
            st = self.stage(dx, dy)
            self.total(st, dx, dy, (LOW, HIGH)[h], self.rh.at[self.k, dx], *extra)
            self.total(st, dx, dy, (LOW, HIGH)[1 - h], *extra)
            self.full[dx, h] = remote(st, self.rf.at[self.k, dx, h], (y_up, y_dn)[h])

        def last(self, dx, *extra):
            for h in range(2):
                self.full[dx, h].wait_recv()
            f = self.rf
            self.total(self.stage(dx, 0), dx, 0, (0, D), f.at[self.k, dx, 0], f.at[self.k, dx, 1], *extra)

    cross, side, back = {}, {}, []

    def y_product(k, cols):
        return dot(act[chunk(k), :], wout[:, cols])

    def d_product(k, cols):
        return dot_t(dpre[chunk(k), :], win[cols, :])

    def d_cross(k, dy):
        r = d[k]
        r.twins()
        st = r.stage(1, dy)
        if dy == 2:
            r.total(st, 1, 2, (0, D))
            cross[k, 2] = remote(st.at[:, span(MIDDLE)], rx_d.at[k, 2, :, span(MIDDLE)], x_nb)
            for h, cols, peer in ((0, FIRST, y_dn), (1, LAST, y_up)):
                side[k, h] = remote(st.at[:, span(cols)], rq_d.at[k, h, :, span(cols)], peer)
            return
        if dy == 0:
            r.total(st, 1, 0, (0, D))
        elif dy == 3:
            side[k, 0].wait_recv()
            r.total(st, 1, 3, FIRST, rq_d.at[k, 0])
            r.total(st, 1, 3, MIDDLE)
            r.total(st, 1, 3, LAST)
        else:
            side[k, 1].wait_recv()
            r.total(st, 1, 1, LAST, rq_d.at[k, 1])
            r.total(st, 1, 1, FIRST)
            r.total(st, 1, 1, MIDDLE)
        cross[k, dy] = remote(st, rx_d.at[k, dy], x_nb)

    def y_cross(k):
        yy[k].last(1)
        cross[k, "y"] = remote(yy[k].stage(1, 0), rx_y.at[k], x_nb)

    def y_done(k):
        cross[k, "y"].wait_recv()
        yy[k].last(0, rx_y.at[k])

    def d_done(k):
        cross[k, 0].wait_recv()
        d[k].last(0, rx_d.at[k, 0])

    def give_back(k):
        parts = [st_y[k, 0, :, pl.ds(c * PART, PART)] for c in range(4)]
        parts += [st_d[k, 0, :, pl.ds(c * PART, PART)] for c in range(4)]
        flat = dot_l(unfold, jnp.concatenate(parts, axis=0)).astype(bf)
        r_send[pl.ds(8 * k, 8)] = flat.reshape(8, 16, PART)
        if k == 0:
            r_recv[ex] = r_send[0]
        for j in range(8 * k, 8 * k + 8):
            if j:
                dz, f = SLOTS[j]
                back.append(remote(r_send.at[j], r_recv.at[ex], slot_peer(8 - dz, f)))

    def grad_out(part):
        @pl.loop(0, 2)
        def _(n):
            cols = pl.ds(pl.multiple_of(part * 1024 + n * TILE, TILE), TILE)
            gout[0, :, cols] = dot_l(act[...], gg[:, cols]).astype(bf)

    def grad_in(part):
        @pl.loop(0, 2)
        def _(n):
            cols = pl.ds(pl.multiple_of(part * 1024 + n * TILE, TILE), TILE)
            gin[0, cols, :] = dot_l(xg[:, cols], dpre[...]).astype(bf)

    def weights():
        w1.wait()
        w2.wait()

    g = [Gather(k) for k in range(2)]
    yy = [Reduce(k, own_y, far_y, sb_y, st_y, rh_y, rf_y) for k in range(2)]
    d = [Reduce(k, own_d, far_d, sb_d, st_d, rh_d, rf_d) for k in range(2)]

    step = {"w": weights}
    for k in range(2):
        for name, call in (
            ("s", lambda k: deal_out(k)),
            ("a", lambda k: g[k].arrive()),
            ("X", lambda k: g[k].whole(xg)),
            ("G", lambda k: g[k].whole(gg)),
            ("hx", hidden_x),
            ("hg", hidden_g),
            ("my0", lambda k: yy[k].make(0, y_product)),
            ("my1", lambda k: yy[k].make(1, y_product)),
            ("md0", lambda k: d[k].make(0, d_product)),
            ("md1", lambda k: d[k].make(1, d_product)),
            ("yf0", lambda k: yy[k].send_far(0)),
            ("yf1", lambda k: yy[k].send_far(1)),
            ("df", lambda k: d[k].send_far(0)),
            ("yn00", lambda k: yy[k].send_near(0, 0)),
            ("yn01", lambda k: yy[k].send_near(0, 1)),
            ("yn10", lambda k: yy[k].send_near(1, 0)),
            ("yn11", lambda k: yy[k].send_near(1, 1)),
            ("dn0", lambda k: d[k].send_near(0, 0)),
            ("dn1", lambda k: d[k].send_near(0, 1)),
            ("dx0", lambda k: d_cross(k, 0)),
            ("dx1", lambda k: d_cross(k, 1)),
            ("dx2", lambda k: d_cross(k, 2)),
            ("dx3", lambda k: d_cross(k, 3)),
            ("yx", y_cross),
            ("y", y_done),
            ("d", d_done),
            ("b", give_back),
        ):
            step[name + ".%d" % k] = (lambda call, k: lambda: call(k))(call, k)
        for ref, letter in ((xg, "x"), (gg, "g")):
            for dx in range(2):
                for dy in range(4):
                    step["%s%d%d.%d" % (letter, dx, dy, k)] = (
                        lambda k, ref, dx, dy: lambda: g[k].take(ref, dx, dy)
                    )(k, ref, dx, dy)
    for part in range(4):
        step["go%d" % part] = (lambda part: lambda: grad_out(part))(part)
        step["gi%d" % part] = (lambda part: lambda: grad_in(part))(part)

    for name in ORDER:
        step[name]()
    assert count[0] == COPIES, count[0]
    for sent in started:
        sent.wait_recv()
    home = dot(taken, r_recv[...].reshape(256, PART)).astype(bf)
    for c in range(4):
        out_ref[:, pl.ds(c * PART, PART)] = home[c * 32:(c + 1) * 32]
        dtok_ref[:, pl.ds(c * PART, PART)] = home[128 + c * 32:128 + (c + 1) * 32]
    for sent in started:
        sent.copy.wait_send()


ORDER = (
    "s.0", "s.1", "a.0", "x10.0", "g01.0", "g03.0", "x03.0", "x01.0", "x11.0", "x13.0", "g11.0", "g02.0",
    "g13.0", "a.1", "x02.0", "g10.0", "x12.0", "g12.0", "X.0", "w", "hx.0", "G.0", "hg.0", "x10.1",
    "g01.1", "md0.0", "g03.1", "md1.0", "x03.1", "my1.0", "x01.1", "my0.0", "dx2.0", "x11.1", "g11.1",
    "x13.1", "g02.1", "g10.1", "g13.1", "yf1.0", "dx1.0", "yf0.0", "x02.1", "dx3.0", "dx0.0", "df.0",
    "x12.1", "g12.1", "X.1", "hx.1", "yn11.0", "G.1", "yn10.0", "hg.1", "yn01.0", "my1.1", "dn0.0",
    "md1.1", "dn1.0", "md0.1", "yx.0", "yn00.0", "my0.1", "dx2.1", "yf1.1", "yf0.1", "dx3.1", "df.1",
    "gi2", "dx1.1", "yn11.1", "yn10.1", "yn00.1", "dn1.1", "dx0.1", "yn01.1", "d.0", "gi1", "gi3", "y.0",
    "dn0.1", "yx.1", "go0", "b.0", "go2", "d.1", "y.1", "b.1", "go3", "go1", "gi0",
)

COPIES = 2 * 15 + 2 * (19 + 16 + 23)


def body(tokens, assign, w_in, w_out, cotangent):
    bf, f32 = jnp.bfloat16, jnp.float32
    vmem = pl.BlockSpec(memory_space=pltpu.VMEM)
    hbm = pl.BlockSpec(memory_space=pltpu.HBM)
    v = pltpu.VMEM
    shapes = tuple(jax.ShapeDtypeStruct(a.shape, bf) for a in (tokens, tokens, w_in, w_out))
    return pl.pallas_call(
        kernel,
        out_shape=shapes,
        in_specs=[hbm] * 5,
        out_specs=(vmem,) * 4,
        scratch_shapes=[
            v((1, 32), jnp.int32), v((256, PART), bf),
            v((EXPERTS, 16, PART), bf), v((EXPERTS, 16, PART), bf),
            v((EXPERTS, 16, PART), bf), v((EXPERTS, 16, PART), bf),
            v((512, D), bf), v((512, D), bf),
            v((D, HID), bf), v((HID, D), bf),
            v((2, 128, D), f32), v((2, 128, D), f32),
            v((2, 128, D), bf), v((2, 128, D), bf),
            v((2, 128, D), bf), v((2, 128, D), bf),
            v((2, 8, 16, D), bf), v((2, 8, 16, D), bf),
            v((2, 2, 16, D), bf), v((2, 2, 2, 16, D), bf), v((2, 16, D), bf),
            v((2, 1, 16, D), bf), v((2, 1, 2, 16, D), bf), v((2, 4, 16, D), bf), v((2, 2, 16, D), bf),
            v((512, HID), bf), v((512, HID), bf),
            v((256, HID), f32), v((256, HID), f32),
            pltpu.SemaphoreType.DMA((COPIES,)),
            pltpu.SemaphoreType.DMA((COPIES,)),
            pltpu.SemaphoreType.DMA((11,)),
        ],
        compiler_params=pltpu.CompilerParams(
            collective_id=0, has_side_effects=True, vmem_limit_bytes=47 * 2**20
        ),
        cost_estimate=pl.CostEstimate(
            flops=12 * 512 * D * HID, bytes_accessed=10 * 2**20, transcendentals=512 * HID
        ),
    )(assign, tokens, cotangent, w_in, w_out)


def solution(mesh):
    in_specs = (
        P(("dp", "expert"), None),
        P(("dp", "expert"), None),
        P("expert", None, "dp"),
        P("expert", "dp", None),
        P(("dp", "expert"), None),
    )
    out_specs = (
        P(("dp", "expert"), None),
        P(("dp", "expert"), None),
        P("expert", None, "dp"),
        P("expert", "dp", None),
    )
    return jax.shard_map(body, mesh=mesh, in_specs=in_specs, out_specs=out_specs, check_vma=False)
```

time: 274 us -> 97.2 us (0.35)
  waiting for transfers between devices: 165 us -> 0 us
  Pallas kernels: 0 us -> 88.6 us
  blocking collectives: 37.8 us -> 0 us
  matrix products: 27.9 us -> 0 us
  between operations: 13.9 us -> 0.65 us
  starting transfers between devices: 13.1 us -> 0 us
  other arithmetic: 7.39 us -> 0 us
    reduce_scatter x1 -> x0, waiting for transfers between devices: 99.2 us -> none  [body(): lax.psum_scatter(jnp.concatenate([out_term, dx_term], axis=1), 'dp', scat...]
    pallas_call x0 -> x1, Pallas kernels: none -> 88.6 us  [body(): pl.pallas_call(kernel, out_shape=shapes, in_specs=[hbm] * 5, out_specs=(v...]
    all_gather x2 -> x0, waiting for transfers between devices: 55.1 us -> none  [the longest x1 33.4 us: body(): lax.all_gather(sent_g, 'dp', axis=0, tiled=True)]
    all_to_all x2 -> x0, blocking collectives: 37.8 us -> none  [the longest x1 23.4 us: body(): lax.all_to_all(dealt_x, 'expert', split_axis=0, concat_axis=0, tiled=True)]
    dot_general x10 -> x0, matrix products: 27.9 us -> none  [the longest x1 4.82 us: body(): lax.dot_general(act, rows_g, (((0,), (0,)), ((), ())), preferred_element_...]
    all_to_all x2 -> x0, starting transfers between devices: 13 us -> none  [the longest x1 9.25 us: body(): lax.all_to_all(dx_rows, 'expert', split_axis=0, concat_axis=0, tiled=True)]
    all_to_all x2 -> x0, waiting for transfers between devices: 10.6 us -> none  [the longest x1 5.41 us: body(): lax.all_to_all(dx_rows, 'expert', split_axis=0, concat_axis=0, tiled=True)]
    concatenate x1 -> x0, other arithmetic: 6.12 us -> none  [body(): jnp.concatenate([out_term, dx_term], axis=1)]
  transfers between devices with their start and end apart: 5 -> 0, of which waited for: 5 -> 0; matrix products, arithmetic and copies ran while one was open for 8% -> 0% of each run, Pallas kernels for 0% -> 0%
where the time goes in v2:
time: 97.2 us; the launch traced here: 95.8 us
  Pallas kernels  88.6 us (91%)
  local copies, waits for them, and re-layouts  6.59 us (7%)
    pallas_call x1, Pallas kernels, body(): pl.pallas_call(kernel, out_shape=shapes, in_specs=[hbm] * 5, out_specs=(v...  88.6 us
    unnamed x10, local copies, waits for them, and re-layouts  6.59 us

profile of v2, /device:TPU:1, one launch (start us, length us, event | category | flops | bytes accessed | tf_op | source)
XLA Modules:
  0.0 95.8 jit_solution(15615729054111893629)
XLA Ops:
  0.6 0.0 copy-start
  0.6 0.9 copy-done
  1.6 0.0 copy-start.1
  1.6 0.9 copy-done.1
  2.5 0.0 copy-start.2
  2.5 0.7 copy-done.2
  3.2 88.6 %shard_map.84 = (bf16[32,4096]{1,0:T(8,128)(2,1)S(1)}, bf16[32,4096]{1,0:T(8,128)(2,1)S(1)}, bf16[1,4096,256]{2,1,0:T(8,128)(2,1)S(1)}, bf16[1,256,4096]{2,1,0:T(8,128)(2,1)S(1)}) custom-call(s32[1,32]{1,0:T(1,128)S(1)} %copy-done.2, bf16[32,4096]{1,0:T(8,128)(2,1)S(1)} %copy-done, bf16[32,4096]{1,0:T(8,128)(2,1)S(1)} %copy-done.1, ...), custom_call_target="tpu_custom_call" | custom-call | flops 6442450944 | bytes 10485760 | tf_op jit(solution)/shard_map/pallas_call | solution.py:437
  91.8 0.7 copy.13
  92.5 0.7 copy.14
  93.2 1.3 %copy.15 = bf16[1,4096,256]{2,1,0:T(8,128)(2,1)} copy(bf16[1,4096,256]{2,1,0:T(8,128)(2,1)S(1)} %get-tuple-element.10) | data formatting | bytes 4194304
  94.5 1.3 %copy.16 = bf16[1,256,4096]{2,1,0:T(8,128)(2,1)} copy(bf16[1,256,4096]{2,1,0:T(8,128)(2,1)S(1)} %get-tuple-element.11) | data formatting | bytes 4194304
Async XLA Ops:
  0.6 1.0 copy-start
  1.6 0.9 copy-start.1
  2.5 0.7 copy-start.2

commit v3 on v2

--- a/solution.py
+++ b/solution.py
@@ -9,7 +9,8 @@
 D = 4096
 HID = 256
 TILE = 512
-PART = 1024
+PART = 512
+WIDE = 1024
 EXPERTS = 16
 SLOTS = [(0, 0), (0, 1), (1, 0), (1, 1), (7, 0), (7, 1), (2, 0), (6, 1)]
 SLOTS += [(3, 0), (3, 1), (5, 0), (5, 1), (4, 0), (4, 1), (2, 1), (6, 0)]
@@ -29,7 +30,7 @@
 
 
 def kernel(
-    assign_hbm, tok_hbm, cot_hbm, win_hbm, wout_hbm,
+    rows_hbm, win_hbm, wout_hbm,
     out_ref, dtok_ref, gin, gout,
     assign_ref, stack, a_send, a_recv, r_send, r_recv,
     xg, gg, win, wout,
@@ -62,12 +63,13 @@
     for peer in everyone:
         pl.semaphore_signal(bar, inc=1, device_id=peer, device_id_type=MESH)
 
-    load = [pltpu.make_async_copy(assign_hbm, assign_ref, lsem.at[0])]
-    for n in range(8):
-        src = (tok_hbm, cot_hbm)[n // 4].at[:, pl.ds(n % 4 * PART, PART)]
-        load.append(pltpu.make_async_copy(src, stack.at[pl.ds(n * 32, 32), :], lsem.at[1 + n]))
-    w1 = pltpu.make_async_copy(win_hbm.at[0], win, lsem.at[9])
-    w2 = pltpu.make_async_copy(wout_hbm.at[0], wout, lsem.at[10])
+    load = [pltpu.make_async_copy(rows_hbm.at[pl.ds(64, 16), pl.ds(0, 128)], assign_ref, lsem.at[0])]
+    for n in range(16):
+        src = rows_hbm.at[pl.ds(n // 8 * 32, 32), pl.ds(n % 8 * PART, PART)]
+        dst = stack.at[n // 8, pl.ds(n % 8 * 32, 32), :]
+        load.append(pltpu.make_async_copy(src, dst, lsem.at[1 + n]))
+    w1 = pltpu.make_async_copy(win_hbm.at[0], win, lsem.at[17])
+    w2 = pltpu.make_async_copy(wout_hbm.at[0], wout, lsem.at[18])
     for copy in load + [w1, w2]:
         copy.start()
 
@@ -99,15 +101,15 @@
 
     for copy in load:
         copy.wait()
-    spread = jnp.where(iota((32, 256), 0) == iota((32, 256), 1) // 8, 1.0, 0.0).astype(bf)
-    order = jnp.broadcast_to(assign_ref[...].astype(f32), (16, 32)).astype(bf)
-    order = dot(order, spread)[0:1, :]
+    spread = jnp.where(iota((128, 256), 0) == iota((128, 256), 1) // 8, 1.0, 0.0).astype(bf)
+    order = dot(assign_ref[...], spread)[0:1, :]
     row, col = iota((256, 256), 0), iota((256, 256), 1)
     hit = ((row // 32) == (col % 8)) & ((row % 32).astype(f32) == order)
     taken = jnp.where(hit, 1.0, 0.0).astype(bf)
 
-    a_send[...] = dot_l(taken, stack[...]).astype(bf).reshape(EXPERTS, 16, PART)
-    a_recv[0] = a_send[ex]
+    for n in range(2):
+        a_send[n] = dot_l(taken, stack[n]).astype(bf).reshape(EXPERTS, 16, PART)
+        a_recv[n, 0] = a_send[n, ex]
 
     o, i = iota((128, 128), 0), iota((128, 128), 1)
     same = (o // 16 == i % 8) & ((o % 16) // 2 == i // 16) & (o % 2 == (i % 16) // 8)
@@ -117,11 +119,11 @@
 
     deal = {}
 
-    def deal_out(k):
+    def deal_out(k, n):
         for j in range(8 * k, 8 * k + 8):
             if j:
                 peer = slot_peer(*SLOTS[j])
-                deal[j] = remote(a_send.at[peer[1]], a_recv.at[j], peer)
+                deal[n, j] = remote(a_send.at[n, peer[1]], a_recv.at[n, j], peer)
 
     def rows(k, s, dx, dy):
         return pl.ds(k * 256 + s * 128 + (dx * 4 + dy) * 16, 16)
@@ -155,22 +157,23 @@
             self.send(ref, (dx, 0), (dx, 3), y_up)
             self.send(ref, (dx, 0), (dx, 1), y_dn)
 
-        def arrive(self):
+        def arrive(self, n):
             k = self.k
             for j in range(8 * k, 8 * k + 8):
                 if j:
-                    deal[j].wait_recv()
-            flat = a_recv[pl.ds(8 * k, 8)].reshape(128, PART)
+                    deal[n, j].wait_recv()
+            flat = a_recv[n, pl.ds(8 * k, 8)].reshape(128, PART)
             flat = dot(unfold, flat).astype(bf)
-            for c in range(4):
-                xg[rows(k, 0, 0, 0), pl.ds(c * PART, PART)] = flat[c * 16:(c + 1) * 16]
-                gg[rows(k, 0, 0, 0), pl.ds(c * PART, PART)] = flat[64 + c * 16:64 + (c + 1) * 16]
-            self.send(xg, (0, 0), (1, 0), x_nb)
-            self.round_y(gg, 0)
-            self.send(gg, (0, 0), (1, 0), x_nb)
-            self.round_y(xg, 0)
-            self.share(xg, (0, 0))
-            self.share(gg, (0, 0))
+            ref = (xg, gg)[n]
+            for c in range(8):
+                ref[rows(k, 0, 0, 0), pl.ds(c * PART, PART)] = flat[c * 16:(c + 1) * 16]
+            if n == 0:
+                self.send(xg, (0, 0), (1, 0), x_nb)
+                self.round_y(xg, 0)
+            else:
+                self.round_y(gg, 0)
+                self.send(gg, (0, 0), (1, 0), x_nb)
+            self.share(ref, (0, 0))
 
         def take(self, ref, dx, dy):
             self.wait(ref, (dx, dy))
@@ -195,17 +198,17 @@
     def hidden_x(k):
         acc_a[...] = jnp.zeros_like(acc_a)
 
-        @pl.loop(0, D // PART)
+        @pl.loop(0, D // WIDE)
         def _(n):
-            cols = pl.ds(pl.multiple_of(n * PART, PART), PART)
+            cols = pl.ds(pl.multiple_of(n * WIDE, WIDE), WIDE)
             acc_a[...] += dot(xg[chunk(k), cols], win[cols, :])
 
     def hidden_g(k):
         acc_b[...] = jnp.zeros_like(acc_b)
 
-        @pl.loop(0, D // PART)
+        @pl.loop(0, D // WIDE)
         def _(n):
-            cols = pl.ds(pl.multiple_of(n * PART, PART), PART)
+            cols = pl.ds(pl.multiple_of(n * WIDE, WIDE), WIDE)
             acc_b[...] += dot_t(gg[chunk(k), cols], wout[:, cols])
 
         pre = acc_a[...]
@@ -235,9 +238,9 @@
             self.pair.append(remote(self.far.at[k, :, cols], self.sb.at[k, :, cols], twin))
 
         def total(self, dst, dx, dy, cols, *others):
-            @pl.loop(0, cols[1] // PART)
+            @pl.loop(0, cols[1] // WIDE)
             def _(n):
-                at = pl.ds(pl.multiple_of(cols[0] + n * PART, PART), PART)
+                at = pl.ds(pl.multiple_of(cols[0] + n * WIDE, WIDE), WIDE)
                 t = self.own[self.k, block(dx, dy), at] + self.sb[self.k, block(dx, dy), at].astype(f32)
                 for other in others:
                     t = t + other[:, at].astype(f32)
@@ -283,7 +286,7 @@
             f = self.rf
             self.total(self.stage(dx, 0), dx, 0, (0, D), f.at[self.k, dx, 0], f.at[self.k, dx, 1], *extra)
 
-    cross, side, back = {}, {}, []
+    cross, side, back = {}, {}, ([], [])
 
     def y_product(k, cols):
         return dot(act[chunk(k), :], wout[:, cols])
@@ -327,17 +330,23 @@
         cross[k, 0].wait_recv()
         d[k].last(0, rx_d.at[k, 0])
 
-    def give_back(k):
-        parts = [st_y[k, 0, :, pl.ds(c * PART, PART)] for c in range(4)]
-        parts += [st_d[k, 0, :, pl.ds(c * PART, PART)] for c in range(4)]
+    def give_back(k, n):
+        parts = [(st_y, st_d)[n][k, 0, :, pl.ds(c * PART, PART)] for c in range(8)]
         flat = dot_l(unfold, jnp.concatenate(parts, axis=0)).astype(bf)
-        r_send[pl.ds(8 * k, 8)] = flat.reshape(8, 16, PART)
+        r_send[n, pl.ds(8 * k, 8)] = flat.reshape(8, 16, PART)
         if k == 0:
-            r_recv[ex] = r_send[0]
+            r_recv[n, ex] = r_send[n, 0]
         for j in range(8 * k, 8 * k + 8):
             if j:
                 dz, f = SLOTS[j]
-                back.append(remote(r_send.at[j], r_recv.at[ex], slot_peer(8 - dz, f)))
+                back[n].append(remote(r_send.at[n, j], r_recv.at[n, ex], slot_peer(8 - dz, f)))
+
+    def home(n, ref):
+        for copy in back[n]:
+            copy.wait_recv()
+        flat = dot(taken, r_recv[n].reshape(256, PART)).astype(bf)
+        for c in range(8):
+            ref[:, pl.ds(c * PART, PART)] = flat[c * 32:(c + 1) * 32]
 
     def grad_out(part):
         @pl.loop(0, 2)
@@ -359,11 +368,13 @@
     yy = [Reduce(k, own_y, far_y, sb_y, st_y, rh_y, rf_y) for k in range(2)]
     d = [Reduce(k, own_d, far_d, sb_d, st_d, rh_d, rf_d) for k in range(2)]
 
-    step = {"w": weights}
+    step = {"w": weights, "hy": lambda: home(0, out_ref), "hd": lambda: home(1, dtok_ref)}
     for k in range(2):
         for name, call in (
-            ("s", lambda k: deal_out(k)),
-            ("a", lambda k: g[k].arrive()),
+            ("sx", lambda k: deal_out(k, 0)),
+            ("sg", lambda k: deal_out(k, 1)),
+            ("ax", lambda k: g[k].arrive(0)),
+            ("ag", lambda k: g[k].arrive(1)),
             ("X", lambda k: g[k].whole(xg)),
             ("G", lambda k: g[k].whole(gg)),
             ("hx", hidden_x),
@@ -388,7 +399,8 @@
             ("yx", y_cross),
             ("y", y_done),
             ("d", d_done),
-            ("b", give_back),
+            ("by", lambda k: give_back(k, 0)),
+            ("bd", lambda k: give_back(k, 1)),
         ):
             step[name + ".%d" % k] = (lambda call, k: lambda: call(k))(call, k)
         for ref, letter in ((xg, "x"), (gg, "g")):
@@ -406,43 +418,51 @@
     assert count[0] == COPIES, count[0]
     for sent in started:
         sent.wait_recv()
-    home = dot(taken, r_recv[...].reshape(256, PART)).astype(bf)
-    for c in range(4):
-        out_ref[:, pl.ds(c * PART, PART)] = home[c * 32:(c + 1) * 32]
-        dtok_ref[:, pl.ds(c * PART, PART)] = home[128 + c * 32:128 + (c + 1) * 32]
     for sent in started:
         sent.copy.wait_send()
 
 
 ORDER = (
-    "s.0", "s.1", "a.0", "x10.0", "g01.0", "g03.0", "x03.0", "x01.0", "x11.0", "x13.0", "g11.0", "g02.0",
-    "g13.0", "a.1", "x02.0", "g10.0", "x12.0", "g12.0", "X.0", "w", "hx.0", "G.0", "hg.0", "x10.1",
-    "g01.1", "md0.0", "g03.1", "md1.0", "x03.1", "my1.0", "x01.1", "my0.0", "dx2.0", "x11.1", "g11.1",
-    "x13.1", "g02.1", "g10.1", "g13.1", "yf1.0", "dx1.0", "yf0.0", "x02.1", "dx3.0", "dx0.0", "df.0",
-    "x12.1", "g12.1", "X.1", "hx.1", "yn11.0", "G.1", "yn10.0", "hg.1", "yn01.0", "my1.1", "dn0.0",
-    "md1.1", "dn1.0", "md0.1", "yx.0", "yn00.0", "my0.1", "dx2.1", "yf1.1", "yf0.1", "dx3.1", "df.1",
-    "gi2", "dx1.1", "yn11.1", "yn10.1", "yn00.1", "dn1.1", "dx0.1", "yn01.1", "d.0", "gi1", "gi3", "y.0",
-    "dn0.1", "yx.1", "go0", "b.0", "go2", "d.1", "y.1", "b.1", "go3", "go1", "gi0",
+    "sg.0", "sx.0", "ag.0", "sg.1", "ax.0", "g01.0", "sx.1", "g03.0", "x10.0", "g02.0", "ag.1", "x03.0",
+    "g10.0", "x01.0", "x11.0", "g11.0", "x13.0", "g13.0", "ax.1", "x02.0", "g10.1", "w", "x12.0", "g12.0",
+    "g03.1", "g01.1", "X.0", "hx.0", "x10.1", "G.0", "hg.0", "x03.1", "x01.1", "md0.0", "md1.0", "my0.0",
+    "x11.1", "x13.1", "my1.0", "g02.1", "dx2.0", "g13.1", "g11.1", "x02.1", "x12.1", "yf1.0", "yf0.0",
+    "dx1.0", "dx0.0", "dx3.0", "g12.1", "X.1", "hx.1", "df.0", "G.1", "hg.1", "yn10.0", "yn11.0", "my1.1",
+    "my0.1", "yn01.0", "yn00.0", "md0.1", "md1.1", "yf1.1", "gi1", "yx.0", "dx2.1", "yf0.1", "yn10.1",
+    "yn11.1", "dx3.1", "dx1.1", "y.0", "dn1.0", "dn0.0", "go1", "go3", "go2", "df.1", "gi0", "by.0",
+    "yn00.1", "yx.1", "yn01.1", "dx0.1", "gi2", "dn1.1", "d.0", "go0", "bd.0", "dn0.1", "y.1", "by.1",
+    "d.1", "bd.1", "gi3", "hy", "hd",
 )
 
-COPIES = 2 * 15 + 2 * (19 + 16 + 23)
+COPIES = 4 * 15 + 2 * (19 + 16 + 23)
+
+
+def finish(*refs):
+    sem = refs[-1]
+    copies = [pltpu.make_async_copy(refs[n], refs[4 + n], sem.at[n]) for n in range(4)]
+    for copy in copies:
+        copy.start()
+    for copy in copies:
+        copy.wait()
 
 
 def body(tokens, assign, w_in, w_out, cotangent):
     bf, f32 = jnp.bfloat16, jnp.float32
+    order = jnp.pad(assign.astype(bf), ((0, 15), (0, D - 32)))
+    rows = jnp.concatenate([tokens, cotangent, order], axis=0)
     vmem = pl.BlockSpec(memory_space=pltpu.VMEM)
     hbm = pl.BlockSpec(memory_space=pltpu.HBM)
     v = pltpu.VMEM
     shapes = tuple(jax.ShapeDtypeStruct(a.shape, bf) for a in (tokens, tokens, w_in, w_out))
-    return pl.pallas_call(
+    results = pl.pallas_call(
         kernel,
         out_shape=shapes,
-        in_specs=[hbm] * 5,
+        in_specs=[hbm] * 3,
         out_specs=(vmem,) * 4,
         scratch_shapes=[
-            v((1, 32), jnp.int32), v((256, PART), bf),
-            v((EXPERTS, 16, PART), bf), v((EXPERTS, 16, PART), bf),
-            v((EXPERTS, 16, PART), bf), v((EXPERTS, 16, PART), bf),
+            v((16, 128), bf), v((2, 256, PART), bf),
+            v((2, EXPERTS, 16, PART), bf), v((2, EXPERTS, 16, PART), bf),
+            v((2, EXPERTS, 16, PART), bf), v((2, EXPERTS, 16, PART), bf),
             v((512, D), bf), v((512, D), bf),
             v((D, HID), bf), v((HID, D), bf),
             v((2, 128, D), f32), v((2, 128, D), f32),
@@ -455,7 +475,7 @@
             v((256, HID), f32), v((256, HID), f32),
             pltpu.SemaphoreType.DMA((COPIES,)),
             pltpu.SemaphoreType.DMA((COPIES,)),
-            pltpu.SemaphoreType.DMA((11,)),
+            pltpu.SemaphoreType.DMA((19,)),
         ],
         compiler_params=pltpu.CompilerParams(
             collective_id=0, has_side_effects=True, vmem_limit_bytes=47 * 2**20
@@ -463,7 +483,16 @@
         cost_estimate=pl.CostEstimate(
             flops=12 * 512 * D * HID, bytes_accessed=10 * 2**20, transcendentals=512 * HID
         ),
-    )(assign, tokens, cotangent, w_in, w_out)
+    )(rows, w_in, w_out)
+    anywhere = pl.BlockSpec(memory_space=pl.ANY)
+    return pl.pallas_call(
+        finish,
+        out_shape=shapes,
+        in_specs=[anywhere] * 4,
+        out_specs=(anywhere,) * 4,
+        scratch_shapes=[pltpu.SemaphoreType.DMA((4,))],
+        compiler_params=pltpu.CompilerParams(vmem_limit_bytes=2**20),
+    )(*results)
 
 
 def solution(mesh):

time: 97.2 us -> 93 us (0.957); the launches traced: 95.8 us -> 92.9 us
  local copies, waits for them, and re-layouts: 6.59 us -> 0 us
  Pallas kernels: 88.6 us -> 90.5 us
  other arithmetic: 0 us -> 1.73 us
    unnamed x10 -> x0, local copies, waits for them, and re-layouts: 6.59 us -> none
    pallas_call x1 -> x2, Pallas kernels: 88.6 us -> 90.5 us  [the longest x1 88.3 us: body(): pl.pallas_call(kernel, out_shape=shapes, in_specs=[hbm] * 3, out_specs=(v...]
    concatenate x0 -> x1, other arithmetic: none -> 1.07 us  [body(): rows = jnp.concatenate([tokens, cotangent, order], axis=0)]
where the time goes in v3:
time: 93 us; the launch traced here: 92.9 us
  Pallas kernels  90.5 us (97%)
  other arithmetic  1.73 us (2%)
    pallas_call x1, Pallas kernels, body(): pl.pallas_call(kernel, out_shape=shapes, in_specs=[hbm] * 3, out_specs=(v...  88.3 us
    pallas_call x1, Pallas kernels, body(): pl.pallas_call(finish, out_shape=shapes, in_specs=[anywhere] * 4, out_spe...  2.22 us

profile of v3, /device:TPU:1, one launch (start us, length us, event | category | flops | bytes accessed | tf_op | source)
XLA Modules:
  0.0 92.9 jit_solution(3596629650137459864)
XLA Ops:
  0.6 0.7 convert_element_type.5
  1.3 1.1 %fusion.1.rows_hbm = bf16[80,4096]{1,0:T(8,128)(2,1)S(1)} fusion(bf16[1,32]{1,0:T(2,128)(2,1)S(1)} %convert_element_type.5, bf16[32,4096]{1,0:T(8,128)(2,1)} %param.9, bf16[32,4096]{1,0:T(8,128)(2,1)} %param.5), kind=kLoop, calls=%fused_computation.2 | loop fusion | flops 2621440 | bytes 1179712 | tf_op jit(solution)/shard_map/concatenate | solution.py:452
  2.4 88.3 %shard_map.84 = (bf16[32,4096]{1,0:T(8,128)(2,1)S(1)}, bf16[32,4096]{1,0:T(8,128)(2,1)S(1)}, bf16[1,4096,256]{2,1,0:T(8,128)(2,1)S(1)}, bf16[1,256,4096]{2,1,0:T(8,128)(2,1)S(1)}) custom-call(bf16[80,4096]{1,0:T(8,128)(2,1)S(1)} %fusion.1.rows_hbm, bf16[1,4096,256]{2,1,0:T(8,128)(2,1)} %win_hbm.1, bf16[1,256,4096]{2,1,0:T(8,128)(2,1)} %wout_hbm.1), custom_call_target="tpu_custom_call" | custom-call | flops 6442450944 | bytes 10485760 | tf_op jit(solution)/shard_map/pallas_call | solution.py:457
  90.7 2.2 %shard_map.85 = (bf16[32,4096]{1,0:T(8,128)(2,1)}, bf16[32,4096]{1,0:T(8,128)(2,1)}, bf16[1,4096,256]{2,1,0:T(8,128)(2,1)}, bf16[1,256,4096]{2,1,0:T(8,128)(2,1)}) custom-call(bf16[32,4096]{1,0:T(8,128)(2,1)S(1)} %get-tuple-element.8.refs_0_, bf16[32,4096]{1,0:T(8,128)(2,1)S(1)} %get-tuple-element.9.refs_1_, ...), custom_call_target="tpu_custom_call" | custom-call | tf_op jit(solution)/shard_map/pallas_call | solution.py:488

commit v4 on v3

--- a/solution.py
+++ b/solution.py
@@ -32,7 +32,7 @@
 def kernel(
     rows_hbm, win_hbm, wout_hbm,
     out_ref, dtok_ref, gin, gout,
-    assign_ref, stack, a_send, a_recv, r_send, r_recv,
+    assign_ref, taken, stack, a_send, a_recv, r_send, r_recv,
     xg, gg, win, wout,
     own_y, own_d, far_y, far_d, sb_y, sb_d, st_y, st_d,
     rh_y, rf_y, rx_y, rh_d, rf_d, rx_d, rq_d,
@@ -99,27 +99,31 @@
     def iota(shape, dim):
         return lax.broadcasted_iota(jnp.int32, shape, dim)
 
-    for copy in load:
-        copy.wait()
-    spread = jnp.where(iota((128, 256), 0) == iota((128, 256), 1) // 8, 1.0, 0.0).astype(bf)
-    order = dot(assign_ref[...], spread)[0:1, :]
+    spread = jnp.where(iota((256, 128), 0) // 8 == iota((256, 128), 1), 1.0, 0.0).astype(bf)
     row, col = iota((256, 256), 0), iota((256, 256), 1)
-    hit = ((row // 32) == (col % 8)) & ((row % 32).astype(f32) == order)
-    taken = jnp.where(hit, 1.0, 0.0).astype(bf)
-
-    for n in range(2):
-        a_send[n] = dot_l(taken, stack[n]).astype(bf).reshape(EXPERTS, 16, PART)
+    place = jnp.where((row & 7) == lax.shift_right_logical(col, 5), (col & 31).astype(f32), -1.0)
+    o, i = iota((128, 128), 0), iota((128, 128), 1)
+    same = (lax.shift_right_logical(o, 4) == (i & 7)) & ((o & 15) == lax.shift_right_logical(i, 3))
+    unfold = jnp.where(same, 1.0, 0.0).astype(bf)
+    load[0].wait()
+    give = jnp.where(place == dot_t(spread, assign_ref[...])[:, 0:1], 1.0, 0.0).astype(bf)
+    taken[...] = give
+
+    def deal_in(n):
+        for copy in load[1 + 8 * n:9 + 8 * n]:
+            copy.wait()
+        a_send[n] = dot(taken[...], stack[n]).astype(bf).reshape(EXPERTS, 16, PART)
         a_recv[n, 0] = a_send[n, ex]
 
-    o, i = iota((128, 128), 0), iota((128, 128), 1)
-    same = (o // 16 == i % 8) & ((o % 16) // 2 == i // 16) & (o % 2 == (i % 16) // 8)
-    unfold = jnp.where(same, 1.0, 0.0).astype(bf)
+    deal_in(0)
 
     pl.semaphore_wait(bar, len(everyone))
 
     deal = {}
 
     def deal_out(k, n):
+        if k == 0 and n == 1:
+            deal_in(1)
         for j in range(8 * k, 8 * k + 8):
             if j:
                 peer = slot_peer(*SLOTS[j])
@@ -344,7 +348,7 @@
     def home(n, ref):
         for copy in back[n]:
             copy.wait_recv()
-        flat = dot(taken, r_recv[n].reshape(256, PART)).astype(bf)
+        flat = dot_l(taken[...], r_recv[n].reshape(256, PART)).astype(bf)
         for c in range(8):
             ref[:, pl.ds(c * PART, PART)] = flat[c * 32:(c + 1) * 32]
 
@@ -423,15 +427,15 @@
 
 
 ORDER = (
-    "sg.0", "sx.0", "ag.0", "sg.1", "ax.0", "g01.0", "sx.1", "g03.0", "x10.0", "g02.0", "ag.1", "x03.0",
-    "g10.0", "x01.0", "x11.0", "g11.0", "x13.0", "g13.0", "ax.1", "x02.0", "g10.1", "w", "x12.0", "g12.0",
-    "g03.1", "g01.1", "X.0", "hx.0", "x10.1", "G.0", "hg.0", "x03.1", "x01.1", "md0.0", "md1.0", "my0.0",
-    "x11.1", "x13.1", "my1.0", "g02.1", "dx2.0", "g13.1", "g11.1", "x02.1", "x12.1", "yf1.0", "yf0.0",
-    "dx1.0", "dx0.0", "dx3.0", "g12.1", "X.1", "hx.1", "df.0", "G.1", "hg.1", "yn10.0", "yn11.0", "my1.1",
-    "my0.1", "yn01.0", "yn00.0", "md0.1", "md1.1", "yf1.1", "gi1", "yx.0", "dx2.1", "yf0.1", "yn10.1",
-    "yn11.1", "dx3.1", "dx1.1", "y.0", "dn1.0", "dn0.0", "go1", "go3", "go2", "df.1", "gi0", "by.0",
-    "yn00.1", "yx.1", "yn01.1", "dx0.1", "gi2", "dn1.1", "d.0", "go0", "bd.0", "dn0.1", "y.1", "by.1",
-    "d.1", "bd.1", "gi3", "hy", "hd",
+    "sx.0", "sg.0", "ax.0", "ag.0", "sx.1", "w", "sg.1", "x01.0", "x10.0", "g03.0", "g01.0", "ax.1",
+    "x11.0", "x03.0", "g02.0", "x13.0", "g13.0", "ag.1", "g11.0", "x03.1", "x12.0", "x01.1", "x02.0",
+    "x10.1", "g10.0", "X.0", "g01.1", "g12.0", "hx.0", "g03.1", "G.0", "hg.0", "my0.0", "my1.0", "x13.1",
+    "x11.1", "md0.0", "g11.1", "g02.1", "md1.0", "g13.1", "yf0.0", "x12.1", "yf1.0", "x02.1", "g10.1",
+    "dx0.0", "dx2.0", "g12.1", "X.1", "hx.1", "yn01.0", "yn00.0", "G.1", "hg.1", "yn10.0", "yn11.0",
+    "dx3.0", "my1.1", "my0.1", "dx1.0", "md0.1", "md1.1", "yf1.1", "df.0", "yx.0", "dx2.1", "yf0.1",
+    "yn11.1", "yn10.1", "dn0.0", "dx3.1", "dn1.0", "y.0", "go1", "df.1", "dx1.1", "yn01.1", "go0", "go2",
+    "by.0", "yx.1", "yn00.1", "gi0", "d.0", "dn1.1", "dx0.1", "dn0.1", "bd.0", "y.1", "by.1", "gi1", "go3",
+    "d.1", "bd.1", "hy", "gi3", "gi2", "hd",
 )
 
 COPIES = 4 * 15 + 2 * (19 + 16 + 23)
@@ -460,7 +464,7 @@
         in_specs=[hbm] * 3,
         out_specs=(vmem,) * 4,
         scratch_shapes=[
-            v((16, 128), bf), v((2, 256, PART), bf),
+            v((16, 128), bf), v((256, 256), bf), v((2, 256, PART), bf),
             v((2, EXPERTS, 16, PART), bf), v((2, EXPERTS, 16, PART), bf),
             v((2, EXPERTS, 16, PART), bf), v((2, EXPERTS, 16, PART), bf),
             v((512, D), bf), v((512, D), bf),

time: 93 us -> 92.1 us (level)
    pallas_call x1, Pallas kernels: 88.3 us -> 87.3 us  [body(): pl.pallas_call(kernel, out_shape=shapes, in_specs=[hbm] * 3, out_specs=(v...]
where the time goes in v4:
time: 92.1 us; the launch traced here: 91.9 us
  Pallas kernels  89.6 us (97%)
  other arithmetic  1.73 us (2%)
    pallas_call x1, Pallas kernels, body(): pl.pallas_call(kernel, out_shape=shapes, in_specs=[hbm] * 3, out_specs=(v...  87.3 us
    pallas_call x1, Pallas kernels, body(): pl.pallas_call(finish, out_shape=shapes, in_specs=[anywhere] * 4, out_spe...  2.22 us

profile of v4, /device:TPU:1, one launch (start us, length us, event | category | flops | bytes accessed | tf_op | source)
XLA Modules:
  0.0 91.9 jit_solution(10359410266002847345)
XLA Ops:
  0.6 0.7 convert_element_type.5
  1.3 1.1 %fusion.1.rows_hbm = bf16[80,4096]{1,0:T(8,128)(2,1)S(1)} fusion(bf16[1,32]{1,0:T(2,128)(2,1)S(1)} %convert_element_type.5, bf16[32,4096]{1,0:T(8,128)(2,1)} %param.9, bf16[32,4096]{1,0:T(8,128)(2,1)} %param.5), kind=kLoop, calls=%fused_computation.2 | loop fusion | flops 2621440 | bytes 1179712 | tf_op jit(solution)/shard_map/concatenate | solution.py:456
  2.4 87.3 %shard_map.84 = (bf16[32,4096]{1,0:T(8,128)(2,1)S(1)}, bf16[32,4096]{1,0:T(8,128)(2,1)S(1)}, bf16[1,4096,256]{2,1,0:T(8,128)(2,1)S(1)}, bf16[1,256,4096]{2,1,0:T(8,128)(2,1)S(1)}) custom-call(bf16[80,4096]{1,0:T(8,128)(2,1)S(1)} %fusion.1.rows_hbm, bf16[1,4096,256]{2,1,0:T(8,128)(2,1)} %win_hbm.1, bf16[1,256,4096]{2,1,0:T(8,128)(2,1)} %wout_hbm.1), custom_call_target="tpu_custom_call" | custom-call | flops 6442450944 | bytes 10485760 | tf_op jit(solution)/shard_map/pallas_call | solution.py:461
  89.7 2.2 %shard_map.85 = (bf16[32,4096]{1,0:T(8,128)(2,1)}, bf16[32,4096]{1,0:T(8,128)(2,1)}, bf16[1,4096,256]{2,1,0:T(8,128)(2,1)}, bf16[1,256,4096]{2,1,0:T(8,128)(2,1)}) custom-call(bf16[32,4096]{1,0:T(8,128)(2,1)S(1)} %get-tuple-element.8.refs_0_, bf16[32,4096]{1,0:T(8,128)(2,1)S(1)} %get-tuple-element.9.refs_1_, ...), custom_call_target="tpu_custom_call" | custom-call | tf_op jit(solution)/shard_map/pallas_call | solution.py:492

commit v5 on v4

--- a/solution.py
+++ b/solution.py
@@ -15,18 +15,24 @@
 SLOTS = [(0, 0), (0, 1), (1, 0), (1, 1), (7, 0), (7, 1), (2, 0), (6, 1)]
 SLOTS += [(3, 0), (3, 1), (5, 0), (5, 1), (4, 0), (4, 1), (2, 1), (6, 0)]
 LOW, HIGH = (0, 2048), (2048, 2048)
-FIRST, MIDDLE, LAST = (0, 1024), (1024, 2048), (3072, 1024)
+FIRST, MIDDLE, LAST = (0, 768), (768, 2560), (3328, 768)
 
 
 class Sent:
     def __init__(self, copy):
         self.copy = copy
         self.due = True
+        self.held = True
 
     def wait_recv(self):
         if self.due:
             self.copy.wait_recv()
         self.due = False
+
+    def wait_send(self):
+        if self.held:
+            self.copy.wait_send()
+        self.held = False
 
 
 def kernel(
@@ -242,9 +248,8 @@
             self.pair.append(remote(self.far.at[k, :, cols], self.sb.at[k, :, cols], twin))
 
         def total(self, dst, dx, dy, cols, *others):
-            @pl.loop(0, cols[1] // WIDE)
-            def _(n):
-                at = pl.ds(pl.multiple_of(cols[0] + n * WIDE, WIDE), WIDE)
+            for c in range(cols[0], cols[0] + cols[1], WIDE):
+                at = pl.ds(c, min(WIDE, cols[0] + cols[1] - c))
                 t = self.own[self.k, block(dx, dy), at] + self.sb[self.k, block(dx, dy), at].astype(f32)
                 for other in others:
                     t = t + other[:, at].astype(f32)
@@ -346,6 +351,9 @@
                 back[n].append(remote(r_send.at[n, j], r_recv.at[n, ex], slot_peer(8 - dz, f)))
 
     def home(n, ref):
+        for sent in started:
+            if sent not in back[0] and sent not in back[1]:
+                sent.wait_send()
         for copy in back[n]:
             copy.wait_recv()
         flat = dot_l(taken[...], r_recv[n].reshape(256, PART)).astype(bf)
@@ -423,7 +431,7 @@
     for sent in started:
         sent.wait_recv()
     for sent in started:
-        sent.copy.wait_send()
+        sent.wait_send()
 
 
 ORDER = (

time: 92.1 us -> 91.4 us (level)
  no operation moved by 1% of the time
where the time goes in v5:
time: 91.4 us; the launch traced here: 91.2 us
  Pallas kernels  88.8 us (97%)
  other arithmetic  1.73 us (2%)
    pallas_call x1, Pallas kernels, body(): pl.pallas_call(kernel, out_shape=shapes, in_specs=[hbm] * 3, out_specs=(v...  86.6 us
    pallas_call x1, Pallas kernels, body(): pl.pallas_call(finish, out_shape=shapes, in_specs=[anywhere] * 4, out_spe...  2.22 us

profile of v5, /device:TPU:1, one launch (start us, length us, event | category | flops | bytes accessed | tf_op | source)
XLA Modules:
  0.0 91.2 jit_solution(6875713742291783476)
XLA Ops:
  0.6 0.7 convert_element_type.5
  1.3 1.1 %fusion.1.rows_hbm = bf16[80,4096]{1,0:T(8,128)(2,1)S(1)} fusion(bf16[1,32]{1,0:T(2,128)(2,1)S(1)} %convert_element_type.5, bf16[32,4096]{1,0:T(8,128)(2,1)} %param.9, bf16[32,4096]{1,0:T(8,128)(2,1)} %param.5), kind=kLoop, calls=%fused_computation.2 | loop fusion | flops 2621440 | bytes 1179712 | tf_op jit(solution)/shard_map/concatenate | solution.py:464
  2.4 86.6 %shard_map.84 = (bf16[32,4096]{1,0:T(8,128)(2,1)S(1)}, bf16[32,4096]{1,0:T(8,128)(2,1)S(1)}, bf16[1,4096,256]{2,1,0:T(8,128)(2,1)S(1)}, bf16[1,256,4096]{2,1,0:T(8,128)(2,1)S(1)}) custom-call(bf16[80,4096]{1,0:T(8,128)(2,1)S(1)} %fusion.1.rows_hbm, bf16[1,4096,256]{2,1,0:T(8,128)(2,1)} %win_hbm.1, bf16[1,256,4096]{2,1,0:T(8,128)(2,1)} %wout_hbm.1), custom_call_target="tpu_custom_call" | custom-call | flops 6442450944 | bytes 10485760 | tf_op jit(solution)/shard_map/pallas_call | solution.py:469
  89.0 2.2 %shard_map.85 = (bf16[32,4096]{1,0:T(8,128)(2,1)}, bf16[32,4096]{1,0:T(8,128)(2,1)}, bf16[1,4096,256]{2,1,0:T(8,128)(2,1)}, bf16[1,256,4096]{2,1,0:T(8,128)(2,1)}) custom-call(bf16[32,4096]{1,0:T(8,128)(2,1)S(1)} %get-tuple-element.8.refs_0_, bf16[32,4096]{1,0:T(8,128)(2,1)S(1)} %get-tuple-element.9.refs_1_, ...), custom_call_target="tpu_custom_call" | custom-call | tf_op jit(solution)/shard_map/pallas_call | solution.py:500
